TPU v7x, 512 devices: a whole 4x8x8 slice. The times are simulated.
512 devices in a mesh: dp: 16 (over z_lo, y), tensor: 32 (over x, z_hi, core).
Axes of the slice: x: 4, y: 8, z: 8 (z_hi: 4, z_lo: 2; z = z_hi * 2 + z_lo), core: 2. Of those that a mesh axis runs over, the one named last changes fastest.
Arguments:
- hidden: bfloat16 [2048, 8192], P('dp'), may hold values from -6 to 6
- target: bfloat16 [2048, 8192], P('dp'), may hold values from -15 to 15
- segments: int32 [16, 128], P('dp'), may hold values from 0 to 3, never falling along the last dimension, each value on 1 to 96 neighbouring positions
- head_map: int32 [64], P('tensor'), may hold values from 0 to 7, as said below
- decay_rate: float32 [64], P('tensor'), may hold values from 0.002 to 0.06
- dt_weight: bfloat16 [8192, 64], P('dp', 'tensor'), may hold values from -0.0625 to 0.0625
- teacher_query: bfloat16 [32, 2048, 1024], P('tensor', 'dp'), may hold values from -0.0625 to 0.0625
- teacher_key: bfloat16 [32, 2048, 128], P('tensor', 'dp'), may hold values from -0.0625 to 0.0625
- teacher_value: bfloat16 [32, 2048, 128], P('tensor', 'dp'), may hold values from -0.0625 to 0.0625
- teacher_out: bfloat16 [32, 1024, 2048], P('tensor', None, 'dp'), may hold values from -0.03125 to 0.03125
Outputs:
- layer_out: bfloat16 [2048, 8192], P('dp', 'tensor')
- grad_x: float32 [8192, 8192], P('dp', 'tensor')
- loss: float32 [], replicated
Inputs may be any that keep to these rules, and one draw needn't show every extreme that they name: `head_map`: every teacher key-value head is named by exactly 8 student heads. `segments`: ids never fall along a row; the tokens of one id form one document.
All inputs are finite; a program needn't handle non-finite values.
Results may differ from a plain program's by a relative error of at most 0.034.
Values may be sent and summed in bfloat16 or wider, within the bound.
A program may use at most 64 MiB of HBM per device.

v0:
```python
import jax
import jax.numpy as jnp
from jax import lax
from jax.sharding import PartitionSpec as P


def from_partner(value, axis, apart):
    mask = 2**apart
    pairs = [(source, source ^ mask) for source in range(lax.axis_size(axis))]
    return lax.ppermute(value, axis, pairs)


def trade_halves(query_blocks, out_blocks, section_bit, tensor_index):
    quarters = query_blocks.shape[0]
    upper_side = tensor_index >> section_bit & 1 == 1
    split_shape = (quarters >> section_bit + 1, 2, 1 << section_bit) + query_blocks.shape[1:]
    split_query = query_blocks.reshape(split_shape)
    split_out = out_blocks.reshape(split_shape)
    stacked = jnp.stack((split_query, split_out), axis=0)
    lower_half = stacked[:, :, 0]
    upper_half = stacked[:, :, 1]
    kept_half = jnp.where(upper_side, upper_half, lower_half)
    sent_half = jnp.where(upper_side, lower_half, upper_half)
    received = from_partner(sent_half, "tensor", section_bit)
    new_lower = jnp.where(upper_side, received, kept_half)
    new_upper = jnp.where(upper_side, kept_half, received)
    merged = jnp.stack((new_lower, new_upper), axis=2)
    return (merged[0].reshape(query_blocks.shape), merged[1].reshape(out_blocks.shape))


def mixing_matrix(c_proj, b_proj, step_sizes, rate, seg_row):
    cumulated = jnp.cumsum(rate * step_sizes)
    positions = jnp.arange(seg_row.shape[0])
    visible = (seg_row[:, None] == seg_row[None, :]) & (positions[None, :] <= positions[:, None])
    distance = jnp.where(visible, cumulated[:, None] - cumulated[None, :], 0.0)
    decays = jnp.where(visible, jnp.exp(-distance), 0.0)
    scores = lax.dot_general(
        c_proj, b_proj, (((1,), (1,)), ((), ())), preferred_element_type=jnp.float32
    )
    return scores * decays


def local(
    hidden,
    target,
    segments,
    head_map,
    decay_rate,
    dt_weight,
    teacher_query,
    teacher_key,
    teacher_value,
    teacher_out,
):
    head_width = teacher_key.shape[2]
    rows_block = teacher_key.shape[1]
    heads_here = decay_rate.shape[0]
    block_width = heads_here * head_width
    quarters = teacher_query.shape[2] // block_width
    tensor_index = lax.axis_index("tensor")
    query_blocks = teacher_query[0].reshape(rows_block, quarters, block_width).transpose(1, 0, 2)
    out_blocks = teacher_out[0].reshape(quarters, block_width, rows_block)
    for section_bit in range(quarters.bit_length() - 1):
        query_blocks, out_blocks = trade_halves(query_blocks, out_blocks, section_bit, tensor_index)
    query_rows = query_blocks.reshape(quarters * rows_block, block_width)
    out_local = out_blocks.transpose(0, 2, 1).reshape(quarters * rows_block, block_width)
    key_pieces, value_pieces = (
        lax.all_gather(teacher_key, "tensor", axis=0, tiled=True),
        lax.all_gather(teacher_value, "tensor", axis=0, tiled=True),
    )
    key_list = []
    value_list = []
    for local_head in range(heads_here):
        teacher_head = head_map[local_head] * quarters
        key_list.append(
            lax.dynamic_slice_in_dim(key_pieces, teacher_head, quarters, 0).reshape(
                quarters * rows_block, head_width
            )
        )
        value_list.append(
            lax.dynamic_slice_in_dim(value_pieces, teacher_head, quarters, 0).reshape(
                quarters * rows_block, head_width
            )
        )
    key_rows = jnp.concatenate(key_list, axis=1)
    value_rows = jnp.concatenate(value_list, axis=1)
    tokens_here = hidden.shape[0]
    model_width = hidden.shape[1]
    pieces = (
        lax.all_gather(query_rows, "dp", axis=0, tiled=True),
        lax.all_gather(key_rows, "dp", axis=0, tiled=True),
        lax.all_gather(value_rows, "dp", axis=0, tiled=True),
        lax.all_gather(dt_weight, "dp", axis=0, tiled=True),
    )
    columns = hidden
    sums_query, sums_key, sums_value, sums_step = tuple(
        (
            jnp.dot(columns, weight_piece, preferred_element_type=jnp.float32)
            for weight_piece in pieces
        )
    )
    c_proj = (sums_query * head_width ** (-0.5)).astype(jnp.bfloat16)
    b_proj = sums_key.astype(jnp.bfloat16)
    x_proj = sums_value.astype(jnp.bfloat16)
    step_sizes = jax.nn.softplus(sums_step)
    out_rows = lax.all_gather(out_local, "dp", axis=0, tiled=True)
    head_shape = (tokens_here, heads_here, head_width)
    c_heads = c_proj.reshape(head_shape)
    b_heads = b_proj.reshape(head_shape)
    x_heads = x_proj.reshape(head_shape)
    mixing = jax.vmap(mixing_matrix, in_axes=(1, 1, 1, 0, None))(
        c_heads, b_heads, step_sizes, decay_rate, segments[0]
    )
    source = step_sizes[:, :, None] * x_heads.astype(jnp.float32)
    mixed = (
        jnp.einsum("htj,jhp->thp", mixing, source, precision=lax.Precision.HIGHEST)
        .astype(jnp.bfloat16)
        .reshape(tokens_here, block_width)
    )
    partial_value = lax.dot_general(
        mixed, out_rows, (((1,), (1,)), ((), ())), preferred_element_type=jnp.float32
    )
    tokens_all = tokens_here * lax.axis_size("dp")
    tensor_count = lax.axis_size("tensor")
    share_width = model_width // tensor_count
    layer_full = lax.psum(partial_value.astype(jnp.bfloat16), "tensor")
    residual = layer_full.astype(jnp.float32) - target.astype(jnp.float32)
    squares = jnp.sum(residual * residual)
    loss_value = lax.psum(squares, "dp") / (tokens_all * model_width)
    grad_out = (2.0 * residual / tokens_all).astype(jnp.bfloat16)
    layer_out = lax.dynamic_slice_in_dim(layer_full, tensor_index * share_width, share_width, 1)
    grad_heads = jnp.dot(grad_out, out_rows, preferred_element_type=jnp.float32).astype(
        jnp.bfloat16
    )
    back = jnp.einsum(
        "htj,thp->jhp",
        mixing,
        grad_heads.reshape(head_shape).astype(jnp.float32),
        precision=lax.Precision.HIGHEST,
    )
    grad_source = (
        (step_sizes[:, :, None] * back).astype(jnp.bfloat16).reshape(tokens_here, block_width)
    )
    columns = hidden
    grad_x = lax.psum_scatter(
        lax.dot_general(
            columns, grad_source, (((0,), (0,)), ((), ())), preferred_element_type=jnp.float32
        ).astype(jnp.bfloat16),
        "dp",
        scatter_dimension=0,
        tiled=True,
    ).astype(jnp.float32)
    return (layer_out, grad_x, loss_value)


def solution(mesh):
    in_specs = (
        P("dp", None),
        P("dp", None),
        P("dp", None),
        P("tensor"),
        P("tensor"),
        P("dp", "tensor"),
        P("tensor", "dp", None),
        P("tensor", "dp", None),
        P("tensor", "dp", None),
        P("tensor", None, "dp"),
    )
    out_specs = (P("dp", "tensor"), P("dp", "tensor"), P())
    return jax.shard_map(local, mesh=mesh, in_specs=in_specs, out_specs=out_specs, check_vma=False)
```

profile of v0, /device:TPU:6, one launch (start us, length us, event | category | flops | bytes accessed | tf_op | source)
XLA Modules:
  0.0 847.5 jit_solution(15668036309865659788)
XLA Ops:
  11.1 1.9 collective-permute-start
  13.0 1.5 collective-permute-done
  14.7 6.1 collective-permute-start.1
  20.8 12.2 %collective-permute-done.1 = bf16[2,1,2,128,256]{4,3,2,0,1:T(8,128)(2,1)S(1)} collective-permute-done((bf16[2,1,2,128,256]{4,3,2,0,1:T(8,128)(2,1)S(1)}, bf16[2,1,2,128,256]{4,3,2,0,1:T(8,128)(2,1)S(1)}, u32[]{:S(2)}, u32[]{:S(2)}) %collective-permute-start.1) | collective-permute-done | bytes 262176 | tf_op jit(solution)/shard_map/ppermute | solution.py:10
  35.8 37.8 %all-gather.13.cloned.1.call-done = bf16[32,128,128]{2,1,0:T(8,128)(2,1)} async-done(((bf16[1,128,128]{2,1,0:T(8,128)(2,1)}), bf16[32,128,128]{2,1,0:T(8,128)(2,1)}) %all-gather.13.cloned.1.call-update) | async-done | bytes 1048592 | tf_op jit(solution)/shard_map/all_gather | solution.py:68
  73.7 58.4 %all-gather.7.cloned.1.call-done = bf16[32,128,128]{2,1,0:T(8,128)(2,1)} async-done(((bf16[1,128,128]{2,1,0:T(8,128)(2,1)}), bf16[32,128,128]{2,1,0:T(8,128)(2,1)}) %all-gather.7.cloned.1.call-update) | async-done | bytes 1048592 | tf_op jit(solution)/shard_map/all_gather | solution.py:69
  132.1 1.1 constant_dynamic-slice_fusion.2
  135.9 32.8 %all_gather.21 = bf16[8192,2]{0,1:T(2,128)(2,1)S(1)} all-gather(bf16[512,2]{0,1:T(2,128)(2,1)S(1)} %copy-done.1), channel_id=1, replica_groups=mesh['dp'=16,'tensor'=32] {'dp'}, dimensions={0}, use_global_device_ids=true | all-gather | bytes 34816 | tf_op jit(solution)/shard_map/all_gather | solution.py:93
  169.8 42.9 %all-gather.11.cloned.1.call-done = bf16[8192,256]{1,0:T(8,128)(2,1)} async-done(((bf16[512,256]{1,0:T(8,128)(2,1)}), bf16[8192,256]{1,0:T(8,128)(2,1)}) %all-gather.11.cloned.1.call-update) | async-done | bytes 4194320 | tf_op jit(solution)/shard_map/all_gather | solution.py:90
  212.7 3.5 fusion.4
  216.2 75.5 %all-gather.15.cloned.1.call-done = bf16[8192,256]{1,0:T(8,128)(2,1)} async-done(((bf16[512,256]{1,0:T(8,128)(2,1)}), bf16[8192,256]{1,0:T(8,128)(2,1)}) %all-gather.15.cloned.1.call-update) | async-done | bytes 4194320 | tf_op jit(solution)/shard_map/all_gather | solution.py:91
  291.7 3.5 convolution_convert_fusion.2
  295.4 75.1 %all-gather.9.cloned.1.call-done = bf16[8192,256]{1,0:T(8,128)(2,1)} async-done(((bf16[512,256]{1,0:T(8,128)(2,1)}), bf16[8192,256]{1,0:T(8,128)(2,1)}) %all-gather.9.cloned.1.call-update) | async-done | bytes 4194320 | tf_op jit(solution)/shard_map/all_gather | solution.py:92
  370.5 3.5 fusion.6
  374.4 75.0 %all-gather.17.cloned.1.call-done = bf16[8192,256]{1,0:T(8,128)(2,1)} async-done(((bf16[512,256]{1,0:T(8,128)(2,1)}), bf16[8192,256]{1,0:T(8,128)(2,1)}) %all-gather.17.cloned.1.call-update) | async-done | bytes 4194320 | tf_op jit(solution)/shard_map/all_gather | solution.py:106
  449.4 5.1 convolution_convert_fusion.1
  454.5 281.3 %all-reduce.2.cloned.1.call-done = bf16[128,8192]{1,0:T(8,128)(2,1)} async-done(((bf16[128,8192]{1,0:T(8,128)(2,1)}), bf16[128,8192]{1,0:T(8,128)(2,1)}) %all-reduce.2.cloned.1.call-update) | async-done | bytes 2097168 | tf_op jit(solution)/shard_map/psum | solution.py:126
  735.8 4.2 fusion.5
  740.3 3.2 fusion
  743.5 3.9 multiply_reduce_fusion
  747.5 34.2 %psum.15 = f32[]{:T(128)} all-reduce(f32[]{:T(128)} %multiply_reduce_fusion), channel_id=1, replica_groups=mesh['dp'=16,'tensor'=32] {'dp'}, use_global_device_ids=true, to_apply=%region_4.5 | all-reduce | flops 1 | bytes 8 | tf_op jit(solution)/shard_map/psum | solution.py:129
  782.3 1.5 constant_dynamic-slice_fusion
  783.8 53.9 %reduce-scatter.2.cloned.1.call-done = bf16[512,256]{0,1:T(8,128)(2,1)} async-done(((bf16[8192,256]{0,1:T(8,128)(2,1)}), bf16[512,256]{0,1:T(8,128)(2,1)}) %reduce-scatter.2.cloned.1.call-update) | async-done | bytes 262160 | tf_op jit(solution)/shard_map/reduce_scatter | solution.py:145
  837.7 1.9 copy.95
  (48 shorter events, 10.1 us)
Async XLA Ops:
  7.2 161.5 %copy-start = (bf16[128,8192]{1,0:T(8,128)(2,1)S(1)}, bf16[128,8192]{1,0:T(8,128)(2,1)}, u32[]{:S(2)}) copy-start(bf16[128,8192]{1,0:T(8,128)(2,1)} %param.10) | copy-start | bytes 6291460
  7.2 26.8 %copy-start.3 = (s32[2]{0:T(128)S(1)}, s32[2]{0:T(128)}, u32[]{:S(2)}) copy-start(s32[2]{0:T(128)} %param.13) | copy-start | bytes 28
  7.2 66.5 %all-gather.13.cloned.1.call-start = ((), (), s32[]{:S(2)}) async-start(), calls=%async_computation.4 | async-start | bytes 1081344 | tf_op jit(solution)/shard_map/all_gather | solution.py:68
  7.9 124.2 %all-gather.7.cloned.1.call-start = ((), (), s32[]{:S(2)}) async-start(), calls=%async_computation.1 | async-start | bytes 1081344 | tf_op jit(solution)/shard_map/all_gather | solution.py:69
  8.7 204.0 %all-gather.11.cloned.1.call-start = ((), (), s32[]{:S(2)}) async-start(), calls=%async_computation.3 | async-start | bytes 4456448 | tf_op jit(solution)/shard_map/all_gather | solution.py:90
  11.1 3.4 collective-permute-start
  14.6 121.3 %copy-start.1 = (bf16[512,2]{0,1:T(2,128)(2,1)S(1)}, bf16[512,2]{0,1:T(2,128)(2,1)}, u32[]{:S(2)}) copy-start(bf16[512,2]{0,1:T(2,128)(2,1)} %param.15) | copy-start | bytes 6148
  14.6 154.1 %copy-start.4 = (f32[2]{0:T(128)S(1)}, f32[2]{0:T(128)}, u32[]{:S(2)}) copy-start(f32[2]{0:T(128)} %param.14) | copy-start | bytes 28
  14.7 155.0 %copy-start.2 = (s32[1,128]{1,0:T(1,128)S(1)}, s32[1,128]{1,0:T(1,128)}, u32[]{:S(2)}) copy-start(s32[1,128]{1,0:T(1,128)} %param.12) | copy-start | bytes 1540
  14.7 18.3 %collective-permute-start.1 = (bf16[2,1,2,128,256]{4,3,2,0,1:T(8,128)(2,1)S(1)}, bf16[2,1,2,128,256]{4,3,2,0,1:T(8,128)(2,1)S(1)}, u32[]{:S(2)}, u32[]{:S(2)}) collective-permute-start(bf16[2,1,2,128,256]{4,3,2,0,1:T(8,128)(2,1)S(1)} %fusion.16), channel_id=1, source_target_pairs={{0,2},{1,3},{2,0},{3,1},{4,6},{5,7},{6,4},{7,5},{8,10},{9,11},{10,... | collective-permute-start | bytes 786440 | tf_op jit(solution)/shard_map/ppermute | solution.py:10
  33.9 257.8 %all-gather.15.cloned.1.call-start = ((), (), s32[]{:S(2)}) async-start(), calls=%async_computation.5 | async-start | bytes 4456448 | tf_op jit(solution)/shard_map/all_gather | solution.py:91
  134.0 236.5 %all-gather.9.cloned.1.call-start = ((), (), s32[]{:S(2)}) async-start(), calls=%async_computation.2 | async-start | bytes 4456448 | tf_op jit(solution)/shard_map/all_gather | solution.py:92
  134.8 314.5 %all-gather.17.cloned.1.call-start = ((), (), s32[]{:S(2)}) async-start(), calls=%async_computation.6 | async-start | bytes 4456448 | tf_op jit(solution)/shard_map/all_gather | solution.py:106
  135.8 599.9 %all-reduce.2.cloned.1.call-start = ((), (), s32[]{:S(2)}) async-start(), calls=%async_computation.7 | async-start | bytes 4194304 | tf_op jit(solution)/shard_map/psum | solution.py:126
  454.5 383.2 %reduce-scatter.2.cloned.1.call-start = ((), (), s32[]{:S(2)}) async-start(), calls=%async_computation.8 | async-start | bytes 4456448 | tf_op jit(solution)/shard_map/reduce_scatter | solution.py:145
Sparse Core Ops, SparseCore 0:
  11.2 62.4 all-gather.12
  76.8 55.2 all-gather.6
  134.8 77.8 all-gather.10
  214.6 77.0 all-gather.14
  293.6 76.8 all-gather.8
  372.4 76.8 all-gather.16
  454.6 281.1 all-reduce.1
  743.7 93.9 reduce-scatter.1
where the time goes:
time: 848 us
  waiting for transfers between devices  715 us (84%)
  blocking collectives  67 us (8%)
  matrix products  24.4 us (3%)
  between operations  17.4 us (2%)
    psum x1, waiting for transfers between devices, local(): layer_full = lax.psum(partial_value.astype(jnp.bfloat16), 'tensor')  281 us
    all_gather x1, waiting for transfers between devices, local(): lax.all_gather(key_rows, 'dp', axis=0, tiled=True)  75.5 us
    all_gather x1, waiting for transfers between devices, local(): lax.all_gather(value_rows, 'dp', axis=0, tiled=True)  75.1 us
    all_gather x1, waiting for transfers between devices, local(): out_rows = lax.all_gather(out_local, 'dp', axis=0, tiled=True)  75 us
    all_gather x1, waiting for transfers between devices, local(): lax.all_gather(teacher_value, 'tensor', axis=0, tiled=True)  58.4 us
    reduce_scatter x1, waiting for transfers between devices, local(): lax.psum_scatter(lax.dot_general(columns, grad_source, (((0,), (0,)), (()...  53.9 us
    all_gather x1, waiting for transfers between devices, local(): lax.all_gather(query_rows, 'dp', axis=0, tiled=True)  42.9 us
    all_gather x1, waiting for transfers between devices, local(): lax.all_gather(teacher_key, 'tensor', axis=0, tiled=True)  37.8 us
  transfers between devices with their start and end apart: 10, of which 10 were waited for; matrix products, arithmetic and copies ran while one was open for 3% of the time, Pallas kernels for 0%

commit v1 on v0

v1 whole, which is shorter than its diff:
```python
import jax
import jax.numpy as jnp
from jax import lax
from jax.experimental import pallas as pl
from jax.experimental.pallas import tpu as pltpu
from jax.sharding import PartitionSpec as P

F32 = jnp.float32
BF16 = jnp.bfloat16
MESH = pl.DeviceIdType.MESH
TOK = 128
TOKENS = 2048
WIDTH = 8192
NY = 8
N_SEM = 192


def dot(a, b, **kw):
    return jnp.dot(a, b, preferred_element_type=F32, **kw)


def dot_t(a, b, **kw):
    return lax.dot_general(a, b, (((1,), (1,)), ((), ())), preferred_element_type=F32, **kw)


def kernel(
    hid_any, tgt_any, seg_ref, map_ref, rate_ref, dtw_ref, q_any, k_any, v_any, o_any,
    lo_ref, gx_ref, loss_ref,
    hid, tg, qg, kvg, og, dtb, hx, hs, ht, hg,
    kvacc, kvp, kvr1, kvt, kvs, kvr2, kvall,
    cacc, cp1, cr1, cp2, cr2,
    w2, mix, dtc, yb, ycat,
    lacc, lp, lr1, lt, ls, lr2, lob,
    gob, dacc, dp1, dr1, dp2, dr2, dxb,
    lsa, lsb, lsb1, lsc, lsc2, lring,
    ssem, rsem, lsem,
):
    dp = lax.axis_index("dp")
    tn = lax.axis_index("tensor")
    zl, y = lax.div(dp, 8), lax.rem(dp, 8)
    x, zh, c = lax.div(tn, 8), lax.rem(lax.div(tn, 2), 4), lax.rem(tn, 2)
    zh1, zh0 = lax.div(zh, 2), lax.rem(zh, 2)
    s, q = lax.div(tn, 4), lax.rem(tn, 4)

    def dev(zl_=zl, y_=y, x_=x, zh1_=zh1, zh0_=zh0, c_=c):
        return (zl_ * 8 + y_, x_ * 8 + zh1_ * 4 + zh0_ * 2 + c_)

    def s_dev(s_):
        return dev(x_=lax.div(s_, 2), zh1_=lax.rem(s_, 2))

    flip_zl, flip_c, flip_h = dev(zl_=1 - zl), dev(c_=1 - c), dev(zh0_=1 - zh0)
    flip_zh = dev(zl_=1 - zl, zh0_=1 - zh0)
    flip_h1 = dev(zh1_=1 - zh1)
    line = (flip_h, flip_zl, flip_zh)

    count = [0]
    pending = []

    def sems(n=1):
        first = count[0]
        count[0] += n
        return first

    def rcopy(src, dst, i, target):
        return pltpu.make_async_remote_copy(
            src_ref=src, dst_ref=dst, send_sem=ssem.at[i], recv_sem=rsem.at[i],
            device_id=target, device_id_type=MESH,
        )

    def send(src, dst, i, target):
        copy = rcopy(src, dst, i, target)
        copy.start()
        pending.append(copy)

    def arrived(dst, i):
        rcopy(dst, dst, i, flip_c).wait_recv()

    def column(index):
        return pl.ds(pl.multiple_of(index * 128, 128), 128)

    def stage(src, dst, i):
        copy = pltpu.make_async_copy(src, dst, lsem.at[i])
        copy.start()
        return copy

    hid_in = stage(hid_any, hid, 0)
    key_in = stage(k_any, kvg.at[y, :, pl.ds(0, 128)], 1)
    value_in = stage(v_any, kvg.at[y, :, pl.ds(128, 128)], 2)
    query_in = stage(q_any, qg.at[y], 3)
    out_in = stage(o_any, og.at[y], 4)
    own_target = tgt_any.at[:, column((zl * 8 + s) * 4 + q)]
    target_in = stage(own_target, tg.at[zl], 5)

    lo_t = lax.div(tn, 16)
    lo_s = lax.div(lax.rem(tn, 16), 2)
    lo_q = 2 * lax.rem(tn, 2)

    def lo_source(slot):
        return (lo_t * 8 + y, lo_s * 4 + lo_q + slot)

    perm_from = (lax.rem(lax.div(tn, 2) + 8, 16), 2 * dp + c)
    perm_to = (lax.div(tn, 2), 2 * lax.rem(dp + 8, 16) + c)
    greeted = [dev(y_=lax.rem(y + 1, 8)), dev(y_=lax.rem(y + 7, 8))]
    greeted += [flip_zl, flip_c, flip_h, flip_zh]
    greeted += [s_dev(lax.rem(s + d, 8)) for d in range(1, 8)]

    def zh_dev(d):
        other = lax.rem(zh + d, 4)
        return dev(zh1_=lax.div(other, 2), zh0_=lax.rem(other, 2))

    def x_dev(d):
        return dev(x_=lax.rem(x + d, 4))

    greeted += [zh_dev(d) for d in range(1, 4)]
    greeted += [perm_from, lo_source(0), lo_source(1)]
    barrier = pltpu.get_barrier_semaphore()
    for target in greeted:
        pl.semaphore_signal(barrier, inc=1, device_id=target, device_id_type=MESH)

    dtb[y, pl.ds(pl.multiple_of(zl * 8, 8), 8), :] = dtw_ref[...]
    hid_in.wait()
    for i in range(NY):
        hx[zl, i] = hid[:, column((zl * 8 + i) * 4 + q)]
        hs[i] = hid[:, column(((1 - zl) * 8 + i) * 4 + q)]
    tile = hid[:, pl.ds(pl.multiple_of(tn * 256, 256), 256)]
    ht[...] = tile.astype(F32).T.astype(BF16)
    key_in.wait()
    value_in.wait()
    pl.semaphore_wait(barrier, len(greeted))

    class Ring:
        def __init__(self, part, chunks):
            self.part, self.chunks = part, chunks
            self.base = sems(8 * chunks)

        def live(self, k, d, ch):
            if k < 3:
                return True
            return d == 0 if self.chunks == 1 else d == ch

        def block(self, k, d):
            return lax.rem(y + (8 - k if d == 0 else k), 8)

        def sem(self, k, d, ch):
            return self.base + (k * 2 + d) * self.chunks + ch

        def send(self, k, d, ch):
            ref = self.part(self.block(k, d), ch)
            to = dev(y_=lax.rem(y + (1 if d == 0 else 7), 8))
            send(ref, ref, self.sem(k, d, ch), to)

        def start(self, chunks=None):
            for ch in range(self.chunks):
                for d in range(2):
                    self.send(0, d, ch)

        def step(self, k):
            for ch in range(self.chunks):
                for d in range(2):
                    if self.live(k, d, ch):
                        arrived(self.part(self.block(k + 1, d), ch), self.sem(k, d, ch))
                        if k < 3 and self.live(k + 1, d, ch):
                            self.send(k + 1, d, ch)

    kv_ring = Ring(lambda b, ch: kvg.at[b, pl.ds(ch * 64, 64)], 2)
    q_ring = Ring(lambda b, ch: qg.at[b, pl.ds(ch * 64, 64)], 2)
    o_ring = Ring(lambda b, ch: og.at[b, pl.ds(ch * 512, 512)], 2)
    dt_ring = Ring(lambda b, ch: dtb.at[b, pl.ds(ch * 8, 8)], 2)
    dx_ring = Ring(lambda b, ch: dxb.at[b, ch], 2)
    loss_ring = Ring(lambda b, ch: lring.at[b], 1)

    h_sem, t_sem, dt_sem, p_sem = sems(), sems(), sems(), sems()
    kv_ring.start()
    send(hs, hx.at[zl], h_sem, flip_zl)
    dt_own = dtb.at[y, pl.ds(pl.multiple_of(zl * 8, 8), 8)]
    send(dt_own, dt_own, dt_sem, flip_zl)
    send(ht, hg.at[c, lax.rem(dp + 8, 16)], p_sem, perm_to)
    query_in.wait()
    kv_ring.step(0)
    q_ring.start()
    other_target = tgt_any.at[:, column(((1 - zl) * 8 + s) * 4 + q)]
    send(other_target, tg.at[zl], t_sem, flip_zl)
    kv_ring.step(1)

    def rows_of(i):
        return jnp.concatenate([hx[0, i], hx[1, i]], axis=0)

    kvacc[...] = jnp.zeros_like(kvacc)
    cacc[...] = jnp.zeros_like(cacc)
    dacc[...] = jnp.zeros_like(dacc)
    arrived(hx.at[1 - zl], h_sem)
    kv_ring.step(2)
    arrived(hg.at[c, lax.div(tn, 2)], p_sem)
    hz_sem = sems(3)
    own_tile = hg.at[c, lax.div(tn, 2)]
    for d in range(1, 4):
        send(own_tile, own_tile, hz_sem + d - 1, zh_dev(d))
    arrived(dtb.at[y, pl.ds(pl.multiple_of((1 - zl) * 8, 8), 8)], dt_sem)
    dt_ring.start()
    kv_ring.step(3)

    def kv_step(i, carry):
        kvacc[...] += dot(rows_of(i), kvg[i])
        return carry

    lax.fori_loop(0, NY, kv_step, 0)
    k1_sem, k2_sem, k3_sem, k4_sem = sems(), sems(3), sems(7), sems()
    for zz in range(2):
        kvp[zz] = kvacc[pl.ds(pl.multiple_of(zz * 128 + (1 - c) * 64, 64), 64), :].astype(BF16)
    send(kvp, kvr1, k1_sem, flip_c)
    q_ring.step(0)
    dt_ring.step(0)
    arrived(kvr1, k1_sem)
    for zz in range(2):
        part = kvacc[pl.ds(pl.multiple_of(zz * 128 + c * 64, 64), 64), :] + kvr1[zz].astype(F32)
        kvt[zz] = part
        kvs[zz] = part.astype(BF16)
    send(kvs.at[zl], kvr2.at[0], k2_sem, flip_h)
    send(kvs.at[1 - zl], kvr2.at[1], k2_sem + 1, flip_zl)
    send(kvs.at[1 - zl], kvr2.at[2], k2_sem + 2, flip_zh)

    def q_block(i):
        rows = rows_of(i)
        for j in range(4):
            cacc[j] += dot(rows, qg[i, :, pl.ds(j * 256, 256)])

    def q_pair(k):
        def body(i, carry):
            q_block(lax.rem(y + jnp.where(i == 0, k, 8 - k), 8))
            return carry
        lax.fori_loop(0, 2, body, 0)

    q_block(y)
    hx_sem = sems(3)
    for d in range(1, 4):
        arrived(hg.at[c, x * 4 + lax.rem(zh + 4 - d, 4)], hz_sem + d - 1)
    quad = hg.at[c, pl.ds(x * 4, 4)]
    for d in range(1, 4):
        send(quad, quad, hx_sem + d - 1, x_dev(d))
    dt_ring.step(1)
    q_ring.step(1)
    for j in range(3):
        arrived(kvr2.at[j], k2_sem + j)
    kvall[c, s] = (
        kvt[zl] + kvr2[0].astype(F32) + kvr2[1].astype(F32) + kvr2[2].astype(F32)
    ).astype(BF16)
    own_kv = kvall.at[c, s]
    for d in range(1, 8):
        send(own_kv, own_kv, k3_sem + d - 1, s_dev(lax.rem(s + d, 8)))
    q_pair(1)
    dt_ring.step(2)
    out_in.wait()
    o_ring.start()
    q_ring.step(2)
    q_pair(2)
    dt_ring.step(3)
    for d in range(1, 8):
        arrived(kvall.at[c, lax.rem(s + 8 - d, 8)], k3_sem + d - 1)
    send(kvall.at[c], kvall.at[c], k4_sem, flip_c)

    w2[...] = jnp.zeros_like(w2)
    for m in range(16):
        for j in range(4):
            for h in range(2):
                w2[h:h + 1, pl.ds((m * 4 + j) * 128, 128)] = dtb[
                    m % 8, pl.ds((m // 8) * 8 + h * 4 + j, 1), :
                ]
    q_ring.step(3)
    lax.fori_loop(3, 5, lambda i, carry: (q_block(lax.rem(y + i, 8)), carry)[1], 0)
    q_block(lax.rem(y + 5, 8))

    class Sum8:
        def __init__(self, acc, p1, r1, p2, r2):
            self.acc, self.p1, self.r1, self.p2, self.r2 = acc, p1, r1, p2, r2
            self.s1, self.s2 = sems(), sems(3)

        def first(self):
            for zz in range(2):
                for hh in range(2):
                    self.p1[zz, hh] = self.acc[hh * 2 + 1 - c, pl.ds(zz * 128, 128), :].astype(BF16)
            send(self.p1, self.r1, self.s1, flip_c)

        def second(self):
            arrived(self.r1, self.s1)
            for zz in range(2):
                for hh in range(2):
                    rows = pl.ds(zz * 128, 128)
                    part = self.acc[hh * 2 + c, rows, :] + self.r1[zz, hh].astype(F32)
                    self.acc[hh * 2 + c, rows, :] = part
                    self.p2[zz, hh] = part.astype(BF16)
            send(self.p2.at[1 - zl, 1 - zh0], self.r2.at[2], self.s2 + 2, flip_zh)
            send(self.p2.at[zl, 1 - zh0], self.r2.at[0], self.s2, flip_h)
            send(self.p2.at[1 - zl, zh0], self.r2.at[1], self.s2 + 1, flip_zl)

        def third(self):
            for j in range(3):
                arrived(self.r2.at[j], self.s2 + j)
            own = self.acc[zh0 * 2 + c, pl.ds(pl.multiple_of(zl * 128, 128), 128), :]
            return own + self.r2[0].astype(F32) + self.r2[1].astype(F32) + self.r2[2].astype(F32)

    c_sum = Sum8(cacc, cp1, cr1, cp2, cr2)
    d_sum = Sum8(dacc, dp1, dr1, dp2, dr2)
    c_sum.first()
    o_ring.step(0)
    c_sum.second()

    best = dict(precision=lax.Precision.HIGHEST)
    weights = w2[...].astype(BF16)

    def softplus(v):
        return jnp.maximum(v, 0.0) + jnp.log1p(jnp.exp(-jnp.abs(v)))

    step_col = softplus(dot_t(hid[...], weights))
    step_row = softplus(dot_t(weights, hid[...]))
    dtc[...] = step_col
    rate0, rate1 = rate_ref[0], rate_ref[1]
    n_lane = step_col.shape[1]
    lane = lax.broadcasted_iota(jnp.int32, (TOK, n_lane), 1)
    subl = lax.broadcasted_iota(jnp.int32, (n_lane, TOK), 0)
    at_t = lax.broadcasted_iota(jnp.int32, (TOK, TOK), 0)
    at_j = lax.broadcasted_iota(jnp.int32, (TOK, TOK), 1)
    lower = (at_j <= at_t).astype(F32)
    upper = (at_t <= at_j).astype(F32)
    cs_col = dot(lower, step_col * jnp.where(lane == 0, rate0, rate1), **best)
    cs_row = dot(step_row * jnp.where(subl == 0, rate0, rate1), upper, **best)
    seg_row = jnp.broadcast_to(seg_ref[...].astype(F32), (TOK, TOK))
    visible = (seg_row == seg_row.T) & (at_j <= at_t)
    for h in range(2):
        distance = jnp.where(visible, cs_col[:, h:h + 1] - cs_row[h:h + 1, :], 0.0)
        mix[h] = jnp.where(visible, jnp.exp(-distance), 0.0)

    o_ring.step(1)
    arrived(kvall.at[1 - c], k4_sem)
    y_sem, y2_sem = sems(3), sems()
    c_full = (c_sum.third() * (128 ** -0.5)).astype(BF16)
    for h in range(2):
        head = map_ref[h]
        both = jnp.concatenate([kvall[0, head], kvall[1, head]], axis=0)
        scores = dot_t(c_full[:, h * 128:(h + 1) * 128], both[:, :128])
        mixing = scores * mix[h]
        mix[h] = mixing
        source = dtc[:, h:h + 1] * both[:, 128:].astype(F32)
        yb[c, zl, zh0, :, pl.ds(h * 128, 128)] = dot(mixing, source, **best).astype(BF16)
    own_y = yb.at[c, zl, zh0]
    send(own_y, own_y, y_sem + 2, flip_zh)
    send(own_y, own_y, y_sem, flip_h)
    send(own_y, own_y, y_sem + 1, flip_zl)
    o_ring.step(2)
    arrived(yb.at[c, zl, 1 - zh0], y_sem)
    arrived(yb.at[c, 1 - zl, zh0], y_sem + 1)
    arrived(yb.at[c, 1 - zl, 1 - zh0], y_sem + 2)
    send(yb.at[c], yb.at[c], y2_sem, flip_c)
    hc_sem = sems()
    for d in range(1, 4):
        arrived(hg.at[c, pl.ds(lax.rem(x + 4 - d, 4) * 4, 4)], hx_sem + d - 1)
    o_ring.step(3)
    arrived(yb.at[1 - c], y2_sem)
    send(hg.at[c], hg.at[c], hc_sem, flip_c)
    for zz in range(2):
        for hh in range(2):
            for cc in range(2):
                ycat[pl.ds(zz * 128, 128), pl.ds((hh * 2 + cc) * 256, 256)] = yb[cc, zz, hh]

    l1_sem, l2_sem = sems(3), sems()
    for d in (1, 2, 3, 0):
        at = lax.rem(x + d, 4)

        def l_block(j, carry):
            value = dot(ycat[...], og[at * 2 + j])
            lacc[at * 2 + j] = value
            lp[at * 2 + j] = value.astype(BF16)
            return carry

        lax.fori_loop(0, 2, l_block, 0)
        if d:
            send(lp.at[pl.ds(at * 2, 2)], lr1.at[d - 1], l1_sem + d - 1, x_dev(d))
    for d in range(3):
        arrived(lr1.at[d], l1_sem + d)
    for j in range(2):
        lt[j] = (
            lacc[x * 2 + j]
            + lr1[0, j].astype(F32) + lr1[1, j].astype(F32) + lr1[2, j].astype(F32)
        )
    ls[...] = lt[1 - zh1].astype(BF16)
    send(ls, lr2, l2_sem, flip_h1)
    target_in.wait()
    arrived(tg.at[1 - zl], t_sem)
    arrived(lr2, l2_sem)
    layer = (lt[zh1] + lr2[...].astype(F32)).astype(BF16)
    g1_sem, g2_sem, la_sem, la2_sem = sems(), sems(3), sems(), sems(3)
    squares = jnp.zeros((8, 128), F32)
    for zz in range(2):
        rows = layer[zz * 128:(zz + 1) * 128]
        lob[zz] = rows
        residual = rows.astype(F32) - tg[zz].astype(F32)
        gob[s, zz] = (2.0 * residual / TOKENS).astype(BF16)
        squares += jnp.sum((residual * residual).reshape(16, 8, 128), axis=0)
    lsa[s] = squares
    send(gob.at[s], gob.at[s], g1_sem, flip_h1)
    send(lsa.at[s], lsa.at[s], la_sem, flip_h1)
    arrived(gob.at[2 * x + 1 - zh1], g1_sem)
    pair = gob.at[pl.ds(x * 2, 2)]
    for d in (2, 1, 3):
        send(pair, pair, g2_sem + d - 1, x_dev(d))
    arrived(lsa.at[2 * x + 1 - zh1], la_sem)
    loss_pair = lsa.at[pl.ds(x * 2, 2)]
    for d in range(1, 4):
        send(loss_pair, loss_pair, la2_sem + d - 1, x_dev(d))

    lo_sem = sems(2)
    lo_tn = 16 * zl + 2 * s + lax.div(q, 2)
    slot = lax.rem(q, 2)
    lo_dst = lo_ref.at[:, column(slot)]
    lo_copies = []
    for zz in range(2):
        to = (zz * 8 + y, lo_tn)
        here = (zl == zz) & (lo_tn == tn)
        copy = pltpu.make_async_remote_copy(
            src_ref=lob.at[zz], dst_ref=lo_dst, send_sem=ssem.at[lo_sem + zz],
            recv_sem=rsem.at[lo_sem + slot], device_id=to, device_id_type=MESH,
        )
        lo_copies.append((copy, here))

        @pl.when(here)
        def _():
            lo_ref[:, column(slot)] = lob[zz]

        @pl.when(jnp.logical_not(here))
        def _():
            copy.start()

    def d_pair(at):
        def body(j, carry):
            i = at * 2 + j
            rows = jnp.concatenate([gob[i, 0], gob[i, 1]], axis=0)
            for k in range(4):
                dacc[k] += dot_t(rows, og[i, pl.ds(k * 256, 256), :])
            return carry
        lax.fori_loop(0, 2, body, 0)

    d_pair(x)
    for d in range(1, 4):
        at = lax.rem(x + 4 - d, 4)
        arrived(gob.at[pl.ds(at * 2, 2)], g2_sem + d - 1)
        d_pair(at)
    d_sum.first()
    lb_sem, lc_sem = sems(), sems(3)
    for d in range(1, 4):
        arrived(lsa.at[pl.ds(lax.rem(x + 4 - d, 4) * 2, 2)], la2_sem + d - 1)
    total = lsa[0]
    for i in range(1, 8):
        total += lsa[i]
    lsb[...] = total
    send(lsb, lsb1, lb_sem, flip_c)
    d_sum.second()
    arrived(lsb1, lb_sem)
    lsc[...] = lsb[...] + lsb1[...]
    for j in range(3):
        send(lsc, lsc2.at[j], lc_sem + j, line[j])
    dy = d_sum.third().astype(BF16).astype(F32)
    dx_sem = sems()
    for h in range(2):
        back = dot(mix[h].T, dy[:, h * 128:(h + 1) * 128], **best)
        dxb[y, zl, :, pl.ds(h * 128, 128)] = (dtc[:, h:h + 1] * back).astype(BF16)
    send(dxb.at[y, zl], dxb.at[y, zl], dx_sem, flip_zl)
    for j in range(3):
        arrived(lsc2.at[j], lc_sem + j)
    lring[y] = lsc[...] + lsc2[0] + lsc2[1] + lsc2[2]
    arrived(dxb.at[y, 1 - zl], dx_sem)
    dx_ring.start()
    loss_ring.start()
    arrived(hg.at[1 - c], hc_sem)

    def g_block(i, first=False):
        grads = jnp.concatenate([dxb[i, 0], dxb[i, 1]], axis=0)
        for b in range(2):
            tokens = jnp.concatenate([hg[b, 8 + i], hg[b, i]], axis=1)
            rows = pl.ds(b * 256, 256)
            if first:
                gx_ref[rows, :] = dot(tokens, grads)
            else:
                gx_ref[rows, :] += dot(tokens, grads)

    g_block(y, True)
    for k in range(4):
        dx_ring.step(k)
        loss_ring.step(k)
        g_block(lax.rem(y + 7 - k, 8))
        if k < 3:
            g_block(lax.rem(y + k + 1, 8))
    total = jnp.sum(jnp.sum(lring[...], axis=0), axis=0, keepdims=True)
    total = jnp.sum(total, axis=1, keepdims=True) / (TOKENS * WIDTH)
    loss_ref[...] = jnp.broadcast_to(total, (8, 128))

    for copy in pending:
        copy.wait_send()
    for copy, here in lo_copies:
        @pl.when(jnp.logical_not(here))
        def _():
            copy.wait_send()
    for k in range(2):
        from_dp, from_tn = lo_source(k)
        here = (from_dp == dp) & (from_tn == tn)

        @pl.when(jnp.logical_not(here))
        def _():
            arrived(lo_ref.at[:, pl.ds(k * 128, 128)], lo_sem + k)


def local(
    hidden, target, segments, head_map, decay_rate, dt_weight,
    teacher_query, teacher_key, teacher_value, teacher_out,
):
    steps = dt_weight.astype(F32).T.reshape(8, 128)
    anywhere = pl.BlockSpec(memory_space=pl.ANY)
    vmem = pl.BlockSpec(memory_space=pltpu.VMEM)
    smem = pl.BlockSpec(memory_space=pltpu.SMEM)

    def b(*shape):
        return pltpu.VMEM(shape, BF16)

    def f(*shape):
        return pltpu.VMEM(shape, F32)

    scratch = [
        b(128, 8192), b(2, 128, 128), b(8, 128, 1024), b(8, 128, 256), b(8, 1024, 128),
        f(8, 16, 128), b(2, 8, 128, 128), b(8, 128, 128), b(256, 128), b(2, 16, 256, 128),
        f(256, 256), b(2, 64, 256), b(2, 64, 256), f(2, 64, 256), b(2, 64, 256), b(3, 64, 256),
        b(2, 8, 64, 256),
        f(4, 256, 256), b(2, 2, 128, 256), b(2, 2, 128, 256), b(2, 2, 128, 256), b(3, 128, 256),
        f(16, 8192), f(2, 128, 128), f(128, 16), b(2, 2, 2, 128, 256), b(256, 1024),
        f(8, 256, 128), b(8, 256, 128), b(3, 2, 256, 128), f(2, 256, 128), b(256, 128),
        b(256, 128), b(2, 128, 128),
        b(8, 2, 128, 128), f(4, 256, 256), b(2, 2, 128, 256), b(2, 2, 128, 256),
        b(2, 2, 128, 256), b(3, 128, 256), b(8, 2, 128, 256),
        f(8, 8, 128), f(8, 128), f(8, 128), f(8, 128), f(3, 8, 128), f(8, 8, 128),
        pltpu.SemaphoreType.DMA((N_SEM,)), pltpu.SemaphoreType.DMA((N_SEM,)),
        pltpu.SemaphoreType.DMA((6,)),
    ]
    layer_out, grad_x, loss = pl.pallas_call(
        kernel,
        out_shape=(
            jax.ShapeDtypeStruct((128, 256), BF16),
            jax.ShapeDtypeStruct((512, 256), F32),
            jax.ShapeDtypeStruct((8, 128), F32),
        ),
        in_specs=[anywhere, anywhere, vmem, smem, smem, vmem] + [anywhere] * 4,
        out_specs=(vmem, vmem, vmem),
        scratch_shapes=scratch,
        compiler_params=pltpu.CompilerParams(
            collective_id=0, has_side_effects=True, vmem_limit_bytes=48 * 1024 * 1024
        ),
    )(
        hidden, target, segments, head_map, decay_rate, steps,
        teacher_query[0], teacher_key[0], teacher_value[0], teacher_out[0],
    )
    return layer_out, grad_x, loss[0, 0]


def solution(mesh):
    in_specs = (
        P("dp", None),
        P("dp", None),
        P("dp", None),
        P("tensor"),
        P("tensor"),
        P("dp", "tensor"),
        P("tensor", "dp", None),
        P("tensor", "dp", None),
        P("tensor", "dp", None),
        P("tensor", None, "dp"),
    )
    out_specs = (P("dp", "tensor"), P("dp", "tensor"), P())
    return jax.shard_map(local, mesh=mesh, in_specs=in_specs, out_specs=out_specs, check_vma=False)
```

time: 848 us -> 155 us (0.18)
  the two profiles are of different devices: /device:TPU:6 before, /device:TPU:66 now
where the time goes in v1:
time: 155 us
  Pallas kernels  143 us (92%)
  local copies, waits for them, and re-layouts  10.5 us (7%)
    pallas_call x1, Pallas kernels, local(): pl.pallas_call(kernel, out_shape=(jax.ShapeDtypeStruct((128, 256), BF16),...  143 us
    unnamed x20, local copies, waits for them, and re-layouts  9.98 us

profile of v1, /device:TPU:66, one launch (start us, length us, event | category | flops | bytes accessed | tf_op | source)
XLA Modules:
  0.0 154.8 jit_solution(11359037578344849011)
XLA Ops:
  0.6 0.7 convert_bitcast_fusion
  1.3 0.0 copy-start
  1.3 1.6 %copy-done = bf16[128,8192]{1,0:T(8,128)(2,1)S(1)} copy-done((bf16[128,8192]{1,0:T(8,128)(2,1)S(1)}, bf16[128,8192]{1,0:T(8,128)(2,1)}, u32[]{:S(2)}) %copy-start) | copy-done | bytes 2097176
  2.9 0.0 copy-start.1
  2.9 1.6 %copy-done.1 = bf16[128,8192]{1,0:T(8,128)(2,1)S(1)} copy-done((bf16[128,8192]{1,0:T(8,128)(2,1)S(1)}, bf16[128,8192]{1,0:T(8,128)(2,1)}, u32[]{:S(2)}) %copy-start.1) | copy-done | bytes 2097176
  4.5 0.0 copy-start.2
  4.5 0.9 copy-done.2
  5.5 0.0 copy-start.3
  5.5 0.9 copy-done.3
  6.4 0.0 copy-start.4
  6.4 0.8 copy-done.4
  7.2 0.0 copy-start.5
  7.2 0.8 copy-done.5
  7.9 0.0 copy-start.6
  7.9 0.7 copy-done.6
  8.6 0.0 copy-start.7
  8.6 0.7 copy-done.7
  9.2 0.0 copy-start.8
  9.2 0.7 copy-done.8
  9.9 143.0 %shard_map.121 = (bf16[128,256]{1,0:T(8,128)(2,1)S(1)}, f32[512,256]{1,0:T(8,128)S(1)}, f32[8,128]{1,0:T(8,128)S(1)}) custom-call(bf16[128,8192]{1,0:T(8,128)(2,1)S(1)} %copy-done, bf16[128,8192]{1,0:T(8,128)(2,1)S(1)} %copy-done.1, s32[1,128]{1,0:T(1,128)S(1)} %copy-done.6, s32[2]{0:T(128)S(1)} %copy-done.7, f32[2]{0:T(128)S(1)} %copy-done.8, ...), custom_call_target="tpu_custom_call" | custom-call | tf_op jit(solution)/shard_map/pallas_call | solution.py:540
  152.9 0.5 slice.3
  153.4 0.6 copy.15
  154.0 0.8 copy.16
  (1 shorter events, 0.0 us)
Async XLA Ops:
  1.3 1.6 %copy-start = (bf16[128,8192]{1,0:T(8,128)(2,1)S(1)}, bf16[128,8192]{1,0:T(8,128)(2,1)}, u32[]{:S(2)}) copy-start(bf16[128,8192]{1,0:T(8,128)(2,1)} %hid_any.1) | copy-start | bytes 6291460
  2.9 1.6 %copy-start.1 = (bf16[128,8192]{1,0:T(8,128)(2,1)S(1)}, bf16[128,8192]{1,0:T(8,128)(2,1)}, u32[]{:S(2)}) copy-start(bf16[128,8192]{1,0:T(8,128)(2,1)} %tgt_any.1) | copy-start | bytes 6291460
  4.5 0.9 copy-start.2
  5.5 0.9 copy-start.3
  6.4 0.8 copy-start.4
  7.2 0.8 copy-start.5
  7.9 0.7 copy-start.6
  8.6 0.7 copy-start.7
  9.2 0.7 copy-start.8

commit v2 on v1

--- a/solution.py
+++ b/solution.py
@@ -30,7 +30,7 @@
     kvacc, kvp, kvr1, kvt, kvs, kvr2, kvall,
     cacc, cp1, cr1, cp2, cr2,
     w2, mix, dtc, yb, ycat,
-    lacc, lp, lr1, lt, ls, lr2, lob,
+    lp, lr1, lt, ls, lr2, lob,
     gob, dacc, dp1, dr1, dp2, dr2, dxb,
     lsa, lsb, lsb1, lsc, lsc2, lring,
     ssem, rsem, lsem,
@@ -87,7 +87,7 @@
     key_in = stage(k_any, kvg.at[y, :, pl.ds(0, 128)], 1)
     value_in = stage(v_any, kvg.at[y, :, pl.ds(128, 128)], 2)
     query_in = stage(q_any, qg.at[y], 3)
-    out_in = stage(o_any, og.at[y], 4)
+    out_in = stage(o_any, og.at[:, column(y)], 4)
     own_target = tgt_any.at[:, column((zl * 8 + s) * 4 + q)]
     target_in = stage(own_target, tg.at[zl], 5)
 
@@ -117,15 +117,9 @@
     for target in greeted:
         pl.semaphore_signal(barrier, inc=1, device_id=target, device_id_type=MESH)
 
-    dtb[y, pl.ds(pl.multiple_of(zl * 8, 8), 8), :] = dtw_ref[...]
-    hid_in.wait()
-    for i in range(NY):
-        hx[zl, i] = hid[:, column((zl * 8 + i) * 4 + q)]
-        hs[i] = hid[:, column(((1 - zl) * 8 + i) * 4 + q)]
-    tile = hid[:, pl.ds(pl.multiple_of(tn * 256, 256), 256)]
-    ht[...] = tile.astype(F32).T.astype(BF16)
     key_in.wait()
     value_in.wait()
+    query_in.wait()
     pl.semaphore_wait(barrier, len(greeted))
 
     class Ring:
@@ -150,12 +144,12 @@
             send(ref, ref, self.sem(k, d, ch), to)
 
         def start(self, chunks=None):
-            for ch in range(self.chunks):
+            for ch in range(self.chunks) if chunks is None else chunks:
                 for d in range(2):
                     self.send(0, d, ch)
 
-        def step(self, k):
-            for ch in range(self.chunks):
+        def step(self, k, chunks=None):
+            for ch in range(self.chunks) if chunks is None else chunks:
                 for d in range(2):
                     if self.live(k, d, ch):
                         arrived(self.part(self.block(k + 1, d), ch), self.sem(k, d, ch))
@@ -164,121 +158,103 @@
 
     kv_ring = Ring(lambda b, ch: kvg.at[b, pl.ds(ch * 64, 64)], 2)
     q_ring = Ring(lambda b, ch: qg.at[b, pl.ds(ch * 64, 64)], 2)
-    o_ring = Ring(lambda b, ch: og.at[b, pl.ds(ch * 512, 512)], 2)
+    o_ring = Ring(lambda b, ch: og.at[pl.ds(ch * 512, 512), column(b)], 2)
     dt_ring = Ring(lambda b, ch: dtb.at[b, pl.ds(ch * 8, 8)], 2)
     dx_ring = Ring(lambda b, ch: dxb.at[b, ch], 2)
     loss_ring = Ring(lambda b, ch: lring.at[b], 1)
 
     h_sem, t_sem, dt_sem, p_sem = sems(), sems(), sems(), sems()
     kv_ring.start()
-    send(hs, hx.at[zl], h_sem, flip_zl)
+    q_ring.start()
+    steps = dtw_ref[...].astype(F32)
+    for r in range(8):
+        lanes = slice((r % 4) * 128, (r % 4 + 1) * 128)
+        dtb[y, pl.ds(zl * 8 + r, 1), :] = steps[r // 4:r // 4 + 1, lanes]
     dt_own = dtb.at[y, pl.ds(pl.multiple_of(zl * 8, 8), 8)]
     send(dt_own, dt_own, dt_sem, flip_zl)
+    hid_in.wait()
+    for i in range(NY):
+        hs[:, pl.ds(i * 128, 128)] = hid[:, column(((1 - zl) * 8 + i) * 4 + q)]
+    send(hs, hx.at[zl], h_sem, flip_zl)
+    kv_ring.step(0)
+    tile = hid[:, pl.ds(pl.multiple_of(tn * 256, 256), 256)]
+    ht[...] = tile.astype(F32).T.astype(BF16)
     send(ht, hg.at[c, lax.rem(dp + 8, 16)], p_sem, perm_to)
-    query_in.wait()
-    kv_ring.step(0)
-    q_ring.start()
+    for i in range(NY):
+        hx[zl, :, pl.ds(i * 128, 128)] = hid[:, column((zl * 8 + i) * 4 + q)]
+    q_ring.step(0, [0])
+    kv_ring.step(1)
+    q_ring.step(0, [1])
+
+    def rows_of(i):
+        lanes = column(i)
+        return jnp.concatenate([hx[0, :, lanes], hx[1, :, lanes]], axis=0)
+
+    def q_pair(k):
+        up, down = lax.rem(y + k, 8), lax.rem(y + 8 - k, 8)
+        rows_up, rows_down = rows_of(up), rows_of(down)
+        for j in range(4):
+            lanes = pl.ds(j * 256, 256)
+            cacc[j] += dot(rows_up, qg[up, :, lanes]) + dot(rows_down, qg[down, :, lanes])
+
+    arrived(hx.at[1 - zl], h_sem)
+    arrived(dtb.at[y, pl.ds(pl.multiple_of((1 - zl) * 8, 8), 8)], dt_sem)
+    dt_ring.start()
     other_target = tgt_any.at[:, column(((1 - zl) * 8 + s) * 4 + q)]
     send(other_target, tg.at[zl], t_sem, flip_zl)
-    kv_ring.step(1)
-
-    def rows_of(i):
-        return jnp.concatenate([hx[0, i], hx[1, i]], axis=0)
-
-    kvacc[...] = jnp.zeros_like(kvacc)
-    cacc[...] = jnp.zeros_like(cacc)
-    dacc[...] = jnp.zeros_like(dacc)
-    arrived(hx.at[1 - zl], h_sem)
+    rows = rows_of(y)
+    for j in range(4):
+        cacc[j] = dot(rows, qg[y, :, pl.ds(j * 256, 256)])
+    q_ring.step(1, [0])
     kv_ring.step(2)
-    arrived(hg.at[c, lax.div(tn, 2)], p_sem)
-    hz_sem = sems(3)
-    own_tile = hg.at[c, lax.div(tn, 2)]
-    for d in range(1, 4):
-        send(own_tile, own_tile, hz_sem + d - 1, zh_dev(d))
-    arrived(dtb.at[y, pl.ds(pl.multiple_of((1 - zl) * 8, 8), 8)], dt_sem)
-    dt_ring.start()
+    q_ring.step(1, [1])
+    q_pair(1)
+    dt_ring.step(0)
+    out_in.wait()
+    q_ring.step(2, [0])
     kv_ring.step(3)
-
-    def kv_step(i, carry):
-        kvacc[...] += dot(rows_of(i), kvg[i])
-        return carry
-
-    lax.fori_loop(0, NY, kv_step, 0)
+    q_ring.step(2, [1])
+    o_ring.start()
     k1_sem, k2_sem, k3_sem, k4_sem = sems(), sems(3), sems(7), sems()
+    rows = jnp.concatenate([hx[0], hx[1]], axis=0)
+    kvacc[...] = dot(rows, kvg[...].reshape(1024, 256))
     for zz in range(2):
         kvp[zz] = kvacc[pl.ds(pl.multiple_of(zz * 128 + (1 - c) * 64, 64), 64), :].astype(BF16)
     send(kvp, kvr1, k1_sem, flip_c)
-    q_ring.step(0)
-    dt_ring.step(0)
+    dt_ring.step(1)
     arrived(kvr1, k1_sem)
     for zz in range(2):
         part = kvacc[pl.ds(pl.multiple_of(zz * 128 + c * 64, 64), 64), :] + kvr1[zz].astype(F32)
         kvt[zz] = part
         kvs[zz] = part.astype(BF16)
+    send(kvs.at[1 - zl], kvr2.at[2], k2_sem + 2, flip_zh)
     send(kvs.at[zl], kvr2.at[0], k2_sem, flip_h)
     send(kvs.at[1 - zl], kvr2.at[1], k2_sem + 1, flip_zl)
-    send(kvs.at[1 - zl], kvr2.at[2], k2_sem + 2, flip_zh)
-
-    def q_block(i):
-        rows = rows_of(i)
-        for j in range(4):
-            cacc[j] += dot(rows, qg[i, :, pl.ds(j * 256, 256)])
-
-    def q_pair(k):
-        def body(i, carry):
-            q_block(lax.rem(y + jnp.where(i == 0, k, 8 - k), 8))
-            return carry
-        lax.fori_loop(0, 2, body, 0)
-
-    q_block(y)
-    hx_sem = sems(3)
-    for d in range(1, 4):
-        arrived(hg.at[c, x * 4 + lax.rem(zh + 4 - d, 4)], hz_sem + d - 1)
-    quad = hg.at[c, pl.ds(x * 4, 4)]
-    for d in range(1, 4):
-        send(quad, quad, hx_sem + d - 1, x_dev(d))
-    dt_ring.step(1)
-    q_ring.step(1)
+    q_pair(2)
+    dt_ring.step(2)
+    q_ring.step(3)
     for j in range(3):
         arrived(kvr2.at[j], k2_sem + j)
     kvall[c, s] = (
         kvt[zl] + kvr2[0].astype(F32) + kvr2[1].astype(F32) + kvr2[2].astype(F32)
     ).astype(BF16)
     own_kv = kvall.at[c, s]
-    for d in range(1, 8):
+    for d in (1, 3, 5, 7, 2, 4, 6):
         send(own_kv, own_kv, k3_sem + d - 1, s_dev(lax.rem(s + d, 8)))
-    q_pair(1)
-    dt_ring.step(2)
-    out_in.wait()
-    o_ring.start()
-    q_ring.step(2)
-    q_pair(2)
-    dt_ring.step(3)
-    for d in range(1, 8):
-        arrived(kvall.at[c, lax.rem(s + 8 - d, 8)], k3_sem + d - 1)
-    send(kvall.at[c], kvall.at[c], k4_sem, flip_c)
-
-    w2[...] = jnp.zeros_like(w2)
-    for m in range(16):
-        for j in range(4):
-            for h in range(2):
-                w2[h:h + 1, pl.ds((m * 4 + j) * 128, 128)] = dtb[
-                    m % 8, pl.ds((m // 8) * 8 + h * 4 + j, 1), :
-                ]
-    q_ring.step(3)
-    lax.fori_loop(3, 5, lambda i, carry: (q_block(lax.rem(y + i, 8)), carry)[1], 0)
-    q_block(lax.rem(y + 5, 8))
 
     class Sum8:
         def __init__(self, acc, p1, r1, p2, r2):
             self.acc, self.p1, self.r1, self.p2, self.r2 = acc, p1, r1, p2, r2
             self.s1, self.s2 = sems(), sems(3)
 
-        def first(self):
-            for zz in range(2):
-                for hh in range(2):
-                    self.p1[zz, hh] = self.acc[hh * 2 + 1 - c, pl.ds(zz * 128, 128), :].astype(BF16)
+        def first(self, add):
+            for hh in range(2):
+                part = self.acc[hh * 2 + 1 - c] + add(hh * 2 + 1 - c)
+                for zz in range(2):
+                    self.p1[zz, hh] = part[zz * 128:(zz + 1) * 128].astype(BF16)
             send(self.p1, self.r1, self.s1, flip_c)
+            for hh in range(2):
+                self.acc[hh * 2 + c] += add(hh * 2 + c)
 
         def second(self):
             arrived(self.r1, self.s1)
@@ -300,10 +276,33 @@
 
     c_sum = Sum8(cacc, cp1, cr1, cp2, cr2)
     d_sum = Sum8(dacc, dp1, dr1, dp2, dr2)
-    c_sum.first()
-    o_ring.step(0)
+
+    last = [lax.rem(y + k, 8) for k in (3, 4, 5)]
+    last_rows = [rows_of(i) for i in last]
+
+    def last_q(k):
+        lanes = pl.ds(pl.multiple_of(k * 256, 256), 256)
+        return sum(dot(r, qg[i, :, lanes]) for r, i in zip(last_rows, last))
+
+    c_sum.first(last_q)
+    o_ring.step(0, [0])
     c_sum.second()
-
+    dt_ring.step(3)
+    o_ring.step(0, [1])
+    w2[...] = jnp.zeros_like(w2)
+    for m in range(16):
+        for j in range(4):
+            for h in range(2):
+                w2[h:h + 1, pl.ds((m * 4 + j) * 128, 128)] = dtb[
+                    m % 8, pl.ds((m // 8) * 8 + h * 4 + j, 1), :
+                ]
+
+    hz_sem = sems(3)
+    own_tile = hg.at[c, lax.div(tn, 2)]
+    arrived(own_tile, p_sem)
+    for d in range(1, 4):
+        send(own_tile, own_tile, hz_sem + d - 1, zh_dev(d))
+    o_ring.step(1, [0])
     best = dict(precision=lax.Precision.HIGHEST)
     weights = w2[...].astype(BF16)
 
@@ -329,10 +328,13 @@
         distance = jnp.where(visible, cs_col[:, h:h + 1] - cs_row[h:h + 1, :], 0.0)
         mix[h] = jnp.where(visible, jnp.exp(-distance), 0.0)
 
-    o_ring.step(1)
-    arrived(kvall.at[1 - c], k4_sem)
+    o_ring.step(1, [1])
+    for d in range(1, 8):
+        arrived(kvall.at[c, lax.rem(s + 8 - d, 8)], k3_sem + d - 1)
+    send(kvall.at[c], kvall.at[c], k4_sem, flip_c)
     y_sem, y2_sem = sems(3), sems()
     c_full = (c_sum.third() * (128 ** -0.5)).astype(BF16)
+    arrived(kvall.at[1 - c], k4_sem)
     for h in range(2):
         head = map_ref[h]
         both = jnp.concatenate([kvall[0, head], kvall[1, head]], axis=0)
@@ -341,6 +343,7 @@
         mix[h] = mixing
         source = dtc[:, h:h + 1] * both[:, 128:].astype(F32)
         yb[c, zl, zh0, :, pl.ds(h * 128, 128)] = dot(mixing, source, **best).astype(BF16)
+    hx_sem = sems(3)
     own_y = yb.at[c, zl, zh0]
     send(own_y, own_y, y_sem + 2, flip_zh)
     send(own_y, own_y, y_sem, flip_h)
@@ -352,56 +355,59 @@
     send(yb.at[c], yb.at[c], y2_sem, flip_c)
     hc_sem = sems()
     for d in range(1, 4):
-        arrived(hg.at[c, pl.ds(lax.rem(x + 4 - d, 4) * 4, 4)], hx_sem + d - 1)
+        arrived(hg.at[c, x * 4 + lax.rem(zh + 4 - d, 4)], hz_sem + d - 1)
     o_ring.step(3)
     arrived(yb.at[1 - c], y2_sem)
-    send(hg.at[c], hg.at[c], hc_sem, flip_c)
     for zz in range(2):
         for hh in range(2):
             for cc in range(2):
                 ycat[pl.ds(zz * 128, 128), pl.ds((hh * 2 + cc) * 256, 256)] = yb[cc, zz, hh]
 
-    l1_sem, l2_sem = sems(3), sems()
-    for d in (1, 2, 3, 0):
+    l0_sem, l1_sem, l2_sem = sems(3), sems(3), sems()
+    for d in (2, 1, 3, 0):
         at = lax.rem(x + d, 4)
-
-        def l_block(j, carry):
-            value = dot(ycat[...], og[at * 2 + j])
-            lacc[at * 2 + j] = value
-            lp[at * 2 + j] = value.astype(BF16)
-            return carry
-
-        lax.fori_loop(0, 2, l_block, 0)
+        value = dot(ycat[...], og[:, pl.ds(pl.multiple_of(at * 256, 256), 256)])
         if d:
-            send(lp.at[pl.ds(at * 2, 2)], lr1.at[d - 1], l1_sem + d - 1, x_dev(d))
+            lp[at, 0] = value[:, :128].astype(BF16)
+            lp[at, 1] = value[:, 128:].astype(BF16)
+            send(lp.at[at, 1 - zh1], lr1.at[1, d - 1], l0_sem + d - 1, x_dev(d))
+        else:
+            lt[0] = value[:, :128]
+            lt[1] = value[:, 128:]
+    for d in (2, 1, 3):
+        at = lax.rem(x + d, 4)
+        send(lp.at[at, zh1], lr1.at[0, d - 1], l1_sem + d - 1, x_dev(d))
     for d in range(3):
-        arrived(lr1.at[d], l1_sem + d)
-    for j in range(2):
-        lt[j] = (
-            lacc[x * 2 + j]
-            + lr1[0, j].astype(F32) + lr1[1, j].astype(F32) + lr1[2, j].astype(F32)
-        )
-    ls[...] = lt[1 - zh1].astype(BF16)
+        arrived(lr1.at[1, d], l0_sem + d)
+    ls[...] = (
+        lt[1 - zh1] + lr1[1, 0].astype(F32) + lr1[1, 1].astype(F32) + lr1[1, 2].astype(F32)
+    ).astype(BF16)
     send(ls, lr2, l2_sem, flip_h1)
+    for d in range(3):
+        arrived(lr1.at[0, d], l1_sem + d)
+    near = lt[zh1] + lr1[0, 0].astype(F32) + lr1[0, 1].astype(F32) + lr1[0, 2].astype(F32)
     target_in.wait()
     arrived(tg.at[1 - zl], t_sem)
     arrived(lr2, l2_sem)
-    layer = (lt[zh1] + lr2[...].astype(F32)).astype(BF16)
-    g1_sem, g2_sem, la_sem, la2_sem = sems(), sems(3), sems(), sems(3)
+    layer = (near + lr2[...].astype(F32)).astype(BF16)
+    g1_sem, g2_sem, g3_sem, la_sem, la2_sem = sems(), sems(3), sems(3), sems(), sems(3)
     squares = jnp.zeros((8, 128), F32)
     for zz in range(2):
         rows = layer[zz * 128:(zz + 1) * 128]
         lob[zz] = rows
         residual = rows.astype(F32) - tg[zz].astype(F32)
-        gob[s, zz] = (2.0 * residual / TOKENS).astype(BF16)
+        gob[pl.ds(zz * 128, 128), column(s)] = (2.0 * residual / TOKENS).astype(BF16)
         squares += jnp.sum((residual * residual).reshape(16, 8, 128), axis=0)
     lsa[s] = squares
-    send(gob.at[s], gob.at[s], g1_sem, flip_h1)
+    own_g = gob.at[:, column(s)]
+    send(own_g, own_g, g1_sem, flip_h1)
+    for d in (2, 1, 3):
+        send(own_g, own_g, g2_sem + d - 1, x_dev(d))
     send(lsa.at[s], lsa.at[s], la_sem, flip_h1)
-    arrived(gob.at[2 * x + 1 - zh1], g1_sem)
-    pair = gob.at[pl.ds(x * 2, 2)]
+    next_g = gob.at[:, column(2 * x + 1 - zh1)]
+    arrived(next_g, g1_sem)
     for d in (2, 1, 3):
-        send(pair, pair, g2_sem + d - 1, x_dev(d))
+        send(next_g, next_g, g3_sem + d - 1, x_dev(d))
     arrived(lsa.at[2 * x + 1 - zh1], la_sem)
     loss_pair = lsa.at[pl.ds(x * 2, 2)]
     for d in range(1, 4):
@@ -429,21 +435,30 @@
         def _():
             copy.start()
 
-    def d_pair(at):
-        def body(j, carry):
-            i = at * 2 + j
-            rows = jnp.concatenate([gob[i, 0], gob[i, 1]], axis=0)
+    def d_part(at):
+        lanes = pl.ds(pl.multiple_of(at * 256, 256), 256)
+        rows = gob[:, lanes]
+
+        def part(k):
+            return dot_t(rows, og[pl.ds(pl.multiple_of(k * 256, 256), 256), lanes])
+        return part
+
+    quad = hg.at[c, pl.ds(x * 4, 4)]
+    for d in range(1, 4):
+        send(quad, quad, hx_sem + d - 1, x_dev(d))
+    part = d_part(x)
+    for k in range(4):
+        dacc[k] = part(k)
+    for d in (1, 3, 2):
+        at = lax.rem(x + 4 - d, 4)
+        arrived(gob.at[:, column(at * 2 + zh1)], g2_sem + d - 1)
+        arrived(gob.at[:, column(at * 2 + 1 - zh1)], g3_sem + d - 1)
+        part = d_part(at)
+        if d == 2:
+            d_sum.first(part)
+        else:
             for k in range(4):
-                dacc[k] += dot_t(rows, og[i, pl.ds(k * 256, 256), :])
-            return carry
-        lax.fori_loop(0, 2, body, 0)
-
-    d_pair(x)
-    for d in range(1, 4):
-        at = lax.rem(x + 4 - d, 4)
-        arrived(gob.at[pl.ds(at * 2, 2)], g2_sem + d - 1)
-        d_pair(at)
-    d_sum.first()
+                dacc[k] += part(k)
     lb_sem, lc_sem = sems(), sems(3)
     for d in range(1, 4):
         arrived(lsa.at[pl.ds(lax.rem(x + 4 - d, 4) * 2, 2)], la2_sem + d - 1)
@@ -457,17 +472,21 @@
     lsc[...] = lsb[...] + lsb1[...]
     for j in range(3):
         send(lsc, lsc2.at[j], lc_sem + j, line[j])
+    for d in range(1, 4):
+        arrived(hg.at[c, pl.ds(lax.rem(x + 4 - d, 4) * 4, 4)], hx_sem + d - 1)
+    send(hg.at[c], hg.at[c], hc_sem, flip_c)
     dy = d_sum.third().astype(BF16).astype(F32)
     dx_sem = sems()
     for h in range(2):
         back = dot(mix[h].T, dy[:, h * 128:(h + 1) * 128], **best)
         dxb[y, zl, :, pl.ds(h * 128, 128)] = (dtc[:, h:h + 1] * back).astype(BF16)
     send(dxb.at[y, zl], dxb.at[y, zl], dx_sem, flip_zl)
+    dx_ring.start([zl])
     for j in range(3):
         arrived(lsc2.at[j], lc_sem + j)
     lring[y] = lsc[...] + lsc2[0] + lsc2[1] + lsc2[2]
     arrived(dxb.at[y, 1 - zl], dx_sem)
-    dx_ring.start()
+    dx_ring.start([1 - zl])
     loss_ring.start()
     arrived(hg.at[1 - c], hc_sem)
 
@@ -490,7 +509,7 @@
             g_block(lax.rem(y + k + 1, 8))
     total = jnp.sum(jnp.sum(lring[...], axis=0), axis=0, keepdims=True)
     total = jnp.sum(total, axis=1, keepdims=True) / (TOKENS * WIDTH)
-    loss_ref[...] = jnp.broadcast_to(total, (8, 128))
+    loss_ref[...] = total
 
     for copy in pending:
         copy.wait_send()
@@ -507,12 +526,23 @@
             arrived(lo_ref.at[:, pl.ds(k * 128, 128)], lo_sem + k)
 
 
+def store(lo_in, gx_in, loss_in, lo_out, gx_out, loss_out, sem):
+    moves = [
+        pltpu.make_async_copy(src, dst, sem.at[i])
+        for i, (src, dst) in enumerate(((gx_in, gx_out), (lo_in, lo_out), (loss_in, loss_out)))
+    ]
+    for move in moves:
+        move.start()
+    for move in moves:
+        move.wait()
+
+
 def local(
     hidden, target, segments, head_map, decay_rate, dt_weight,
     teacher_query, teacher_key, teacher_value, teacher_out,
 ):
-    steps = dt_weight.astype(F32).T.reshape(8, 128)
-    anywhere = pl.BlockSpec(memory_space=pl.ANY)
+    steps = dt_weight.T
+    anywhere = pl.BlockSpec(memory_space=pltpu.HBM)
     vmem = pl.BlockSpec(memory_space=pltpu.VMEM)
     smem = pl.BlockSpec(memory_space=pltpu.SMEM)
 
@@ -523,15 +553,15 @@
         return pltpu.VMEM(shape, F32)
 
     scratch = [
-        b(128, 8192), b(2, 128, 128), b(8, 128, 1024), b(8, 128, 256), b(8, 1024, 128),
-        f(8, 16, 128), b(2, 8, 128, 128), b(8, 128, 128), b(256, 128), b(2, 16, 256, 128),
+        b(128, 8192), b(2, 128, 128), b(8, 128, 1024), b(8, 128, 256), b(1024, 1024),
+        f(8, 16, 128), b(2, 128, 1024), b(128, 1024), b(256, 128), b(2, 16, 256, 128),
         f(256, 256), b(2, 64, 256), b(2, 64, 256), f(2, 64, 256), b(2, 64, 256), b(3, 64, 256),
         b(2, 8, 64, 256),
         f(4, 256, 256), b(2, 2, 128, 256), b(2, 2, 128, 256), b(2, 2, 128, 256), b(3, 128, 256),
         f(16, 8192), f(2, 128, 128), f(128, 16), b(2, 2, 2, 128, 256), b(256, 1024),
-        f(8, 256, 128), b(8, 256, 128), b(3, 2, 256, 128), f(2, 256, 128), b(256, 128),
+        b(4, 2, 256, 128), b(2, 3, 256, 128), f(2, 256, 128), b(256, 128),
         b(256, 128), b(2, 128, 128),
-        b(8, 2, 128, 128), f(4, 256, 256), b(2, 2, 128, 256), b(2, 2, 128, 256),
+        b(256, 1024), f(4, 256, 256), b(2, 2, 128, 256), b(2, 2, 128, 256),
         b(2, 2, 128, 256), b(3, 128, 256), b(8, 2, 128, 256),
         f(8, 8, 128), f(8, 128), f(8, 128), f(8, 128), f(3, 8, 128), f(8, 8, 128),
         pltpu.SemaphoreType.DMA((N_SEM,)), pltpu.SemaphoreType.DMA((N_SEM,)),
@@ -542,18 +572,29 @@
         out_shape=(
             jax.ShapeDtypeStruct((128, 256), BF16),
             jax.ShapeDtypeStruct((512, 256), F32),
-            jax.ShapeDtypeStruct((8, 128), F32),
+            jax.ShapeDtypeStruct((1, 1), F32),
         ),
         in_specs=[anywhere, anywhere, vmem, smem, smem, vmem] + [anywhere] * 4,
         out_specs=(vmem, vmem, vmem),
         scratch_shapes=scratch,
         compiler_params=pltpu.CompilerParams(
-            collective_id=0, has_side_effects=True, vmem_limit_bytes=48 * 1024 * 1024
+            collective_id=0, has_side_effects=True, vmem_limit_bytes=65536 * 1024 - 640 * 1024
         ),
     )(
         hidden, target, segments, head_map, decay_rate, steps,
         teacher_query[0], teacher_key[0], teacher_value[0], teacher_out[0],
     )
+    layer_out, grad_x, loss = pl.pallas_call(
+        store,
+        out_shape=(
+            jax.ShapeDtypeStruct((128, 256), BF16),
+            jax.ShapeDtypeStruct((512, 256), F32),
+            jax.ShapeDtypeStruct((1, 1), F32),
+        ),
+        in_specs=[anywhere] * 3,
+        out_specs=(anywhere,) * 3,
+        scratch_shapes=[pltpu.SemaphoreType.DMA((3,))],
+    )(layer_out, grad_x, loss)
     return layer_out, grad_x, loss[0, 0]
 
 

time: 155 us -> 162 us (1.045)
  the two profiles are of different devices: /device:TPU:66 before, /device:TPU:6 now
where the time goes in v2:
time: 162 us; the launch traced here: 159 us
  Pallas kernels  158 us (98%)
    pallas_call x1, Pallas kernels, local(): pl.pallas_call(kernel, out_shape=(jax.ShapeDtypeStruct((128, 256), BF16),...  138 us
    pallas_call x1, Pallas kernels, local(): pl.pallas_call(store, out_shape=(jax.ShapeDtypeStruct((128, 256), BF16),...  19.7 us

profile of v2, /device:TPU:6, one launch (start us, length us, event | category | flops | bytes accessed | tf_op | source)
XLA Modules:
  0.0 158.5 jit_solution(14488502493143967767)
XLA Ops:
  0.6 138.2 %shard_map.121 = (bf16[128,256]{1,0:T(8,128)(2,1)}, f32[512,256]{1,0:T(8,128)}, f32[1,1]{1,0:T(1,128)}) custom-call(bf16[128,8192]{1,0:T(8,128)(2,1)} %hid_any.1, bf16[128,8192]{1,0:T(8,128)(2,1)} %tgt_any.1, s32[1,128]{1,0:T(1,128)} %seg_ref.1, s32[2]{0:T(128)} %map_ref.1, f32[2]{0:T(128)} %rate_ref.1, bf16[2,512]{1,0:T(2,128)(2,1)} %bitcast.10, ...), custom_call_target="tpu_custom_call" | custom-call | tf_op jit(solution)/shard_map/pallas_call | solution.py:570
  138.9 19.7 %shard_map.122 = (bf16[128,256]{1,0:T(8,128)(2,1)}, f32[512,256]{1,0:T(8,128)}, f32[1,1]{1,0:T(1,128)}) custom-call(bf16[128,256]{1,0:T(8,128)(2,1)} %get-tuple-element.9.lo_in, f32[512,256]{1,0:T(8,128)} %get-tuple-element.10.gx_in, f32[1,1]{1,0:T(1,128)} %get-tuple-element.11.loss_in), custom_call_target="tpu_custom_call" | custom-call | tf_op jit(solution)/shard_map/pallas_call | solution.py:587

commit v3 on v2

--- a/solution.py
+++ b/solution.py
@@ -83,6 +83,32 @@
         copy.start()
         return copy
 
+    lo_t = lax.div(tn, 16)
+    lo_s = lax.div(lax.rem(tn, 16), 2)
+    lo_q = 2 * lax.rem(tn, 2)
+
+    def lo_source(slot):
+        return (lo_t * 8 + y, lo_s * 4 + lo_q + slot)
+
+    perm_from = (lax.rem(lax.div(tn, 2) + 8, 16), 2 * dp + c)
+    perm_to = (lax.div(tn, 2), 2 * lax.rem(dp + 8, 16) + c)
+    greeted = [dev(y_=lax.rem(y + 1, 8)), dev(y_=lax.rem(y + 7, 8))]
+    greeted += [flip_zl, flip_c, flip_h, flip_zh]
+    greeted += [s_dev(lax.rem(s + d, 8)) for d in range(1, 8)]
+
+    def zh_dev(d):
+        other = lax.rem(zh + d, 4)
+        return dev(zh1_=lax.div(other, 2), zh0_=lax.rem(other, 2))
+
+    def x_dev(d):
+        return dev(x_=lax.rem(x + d, 4))
+
+    greeted += [zh_dev(d) for d in range(1, 4)]
+    greeted += [perm_from, lo_source(0), lo_source(1)]
+    barrier = pltpu.get_barrier_semaphore()
+    for target in greeted:
+        pl.semaphore_signal(barrier, inc=1, device_id=target, device_id_type=MESH)
+
     hid_in = stage(hid_any, hid, 0)
     key_in = stage(k_any, kvg.at[y, :, pl.ds(0, 128)], 1)
     value_in = stage(v_any, kvg.at[y, :, pl.ds(128, 128)], 2)
@@ -91,32 +117,6 @@
     own_target = tgt_any.at[:, column((zl * 8 + s) * 4 + q)]
     target_in = stage(own_target, tg.at[zl], 5)
 
-    lo_t = lax.div(tn, 16)
-    lo_s = lax.div(lax.rem(tn, 16), 2)
-    lo_q = 2 * lax.rem(tn, 2)
-
-    def lo_source(slot):
-        return (lo_t * 8 + y, lo_s * 4 + lo_q + slot)
-
-    perm_from = (lax.rem(lax.div(tn, 2) + 8, 16), 2 * dp + c)
-    perm_to = (lax.div(tn, 2), 2 * lax.rem(dp + 8, 16) + c)
-    greeted = [dev(y_=lax.rem(y + 1, 8)), dev(y_=lax.rem(y + 7, 8))]
-    greeted += [flip_zl, flip_c, flip_h, flip_zh]
-    greeted += [s_dev(lax.rem(s + d, 8)) for d in range(1, 8)]
-
-    def zh_dev(d):
-        other = lax.rem(zh + d, 4)
-        return dev(zh1_=lax.div(other, 2), zh0_=lax.rem(other, 2))
-
-    def x_dev(d):
-        return dev(x_=lax.rem(x + d, 4))
-
-    greeted += [zh_dev(d) for d in range(1, 4)]
-    greeted += [perm_from, lo_source(0), lo_source(1)]
-    barrier = pltpu.get_barrier_semaphore()
-    for target in greeted:
-        pl.semaphore_signal(barrier, inc=1, device_id=target, device_id_type=MESH)
-
     key_in.wait()
     value_in.wait()
     query_in.wait()
@@ -160,7 +160,7 @@
     q_ring = Ring(lambda b, ch: qg.at[b, pl.ds(ch * 64, 64)], 2)
     o_ring = Ring(lambda b, ch: og.at[pl.ds(ch * 512, 512), column(b)], 2)
     dt_ring = Ring(lambda b, ch: dtb.at[b, pl.ds(ch * 8, 8)], 2)
-    dx_ring = Ring(lambda b, ch: dxb.at[b, ch], 2)
+    dx_ring = Ring(lambda b, ch: dxb.at[b, 1 - zl if ch else zl], 2)
     loss_ring = Ring(lambda b, ch: lring.at[b], 1)
 
     h_sem, t_sem, dt_sem, p_sem = sems(), sems(), sems(), sems()
@@ -208,19 +208,24 @@
     q_ring.step(1, [0])
     kv_ring.step(2)
     q_ring.step(1, [1])
+    hz_sem = sems(3)
+    own_tile = hg.at[c, lax.div(tn, 2)]
+    arrived(own_tile, p_sem)
+    for d in range(1, 4):
+        send(own_tile, own_tile, hz_sem + d - 1, zh_dev(d))
     q_pair(1)
     dt_ring.step(0)
     out_in.wait()
     q_ring.step(2, [0])
     kv_ring.step(3)
-    q_ring.step(2, [1])
-    o_ring.start()
     k1_sem, k2_sem, k3_sem, k4_sem = sems(), sems(3), sems(7), sems()
     rows = jnp.concatenate([hx[0], hx[1]], axis=0)
     kvacc[...] = dot(rows, kvg[...].reshape(1024, 256))
     for zz in range(2):
         kvp[zz] = kvacc[pl.ds(pl.multiple_of(zz * 128 + (1 - c) * 64, 64), 64), :].astype(BF16)
     send(kvp, kvr1, k1_sem, flip_c)
+    q_ring.step(2, [1])
+    o_ring.start()
     dt_ring.step(1)
     arrived(kvr1, k1_sem)
     for zz in range(2):
@@ -230,6 +235,12 @@
     send(kvs.at[1 - zl], kvr2.at[2], k2_sem + 2, flip_zh)
     send(kvs.at[zl], kvr2.at[0], k2_sem, flip_h)
     send(kvs.at[1 - zl], kvr2.at[1], k2_sem + 1, flip_zl)
+    hx_sem = sems(3)
+    for d in range(1, 4):
+        arrived(hg.at[c, x * 4 + lax.rem(zh + 4 - d, 4)], hz_sem + d - 1)
+    quad = hg.at[c, pl.ds(x * 4, 4)]
+    for d in range(1, 4):
+        send(quad, quad, hx_sem + d - 1, x_dev(d))
     q_pair(2)
     dt_ring.step(2)
     q_ring.step(3)
@@ -297,11 +308,6 @@
                     m % 8, pl.ds((m // 8) * 8 + h * 4 + j, 1), :
                 ]
 
-    hz_sem = sems(3)
-    own_tile = hg.at[c, lax.div(tn, 2)]
-    arrived(own_tile, p_sem)
-    for d in range(1, 4):
-        send(own_tile, own_tile, hz_sem + d - 1, zh_dev(d))
     o_ring.step(1, [0])
     best = dict(precision=lax.Precision.HIGHEST)
     weights = w2[...].astype(BF16)
@@ -335,29 +341,32 @@
     y_sem, y2_sem = sems(3), sems()
     c_full = (c_sum.third() * (128 ** -0.5)).astype(BF16)
     arrived(kvall.at[1 - c], k4_sem)
+    mixings = []
     for h in range(2):
         head = map_ref[h]
         both = jnp.concatenate([kvall[0, head], kvall[1, head]], axis=0)
         scores = dot_t(c_full[:, h * 128:(h + 1) * 128], both[:, :128])
         mixing = scores * mix[h]
-        mix[h] = mixing
+        mixings.append(mixing)
         source = dtc[:, h:h + 1] * both[:, 128:].astype(F32)
         yb[c, zl, zh0, :, pl.ds(h * 128, 128)] = dot(mixing, source, **best).astype(BF16)
-    hx_sem = sems(3)
     own_y = yb.at[c, zl, zh0]
     send(own_y, own_y, y_sem + 2, flip_zh)
     send(own_y, own_y, y_sem, flip_h)
     send(own_y, own_y, y_sem + 1, flip_zl)
+    for h in range(2):
+        mix[h] = mixings[h].T
     o_ring.step(2)
     arrived(yb.at[c, zl, 1 - zh0], y_sem)
     arrived(yb.at[c, 1 - zl, zh0], y_sem + 1)
     arrived(yb.at[c, 1 - zl, 1 - zh0], y_sem + 2)
     send(yb.at[c], yb.at[c], y2_sem, flip_c)
     hc_sem = sems()
-    for d in range(1, 4):
-        arrived(hg.at[c, x * 4 + lax.rem(zh + 4 - d, 4)], hz_sem + d - 1)
     o_ring.step(3)
     arrived(yb.at[1 - c], y2_sem)
+    for d in range(1, 4):
+        arrived(hg.at[c, pl.ds(lax.rem(x + 4 - d, 4) * 4, 4)], hx_sem + d - 1)
+    send(hg.at[c], hg.at[c], hc_sem, flip_c)
     for zz in range(2):
         for hh in range(2):
             for cc in range(2):
@@ -443,9 +452,6 @@
             return dot_t(rows, og[pl.ds(pl.multiple_of(k * 256, 256), 256), lanes])
         return part
 
-    quad = hg.at[c, pl.ds(x * 4, 4)]
-    for d in range(1, 4):
-        send(quad, quad, hx_sem + d - 1, x_dev(d))
     part = d_part(x)
     for k in range(4):
         dacc[k] = part(k)
@@ -472,21 +478,18 @@
     lsc[...] = lsb[...] + lsb1[...]
     for j in range(3):
         send(lsc, lsc2.at[j], lc_sem + j, line[j])
-    for d in range(1, 4):
-        arrived(hg.at[c, pl.ds(lax.rem(x + 4 - d, 4) * 4, 4)], hx_sem + d - 1)
-    send(hg.at[c], hg.at[c], hc_sem, flip_c)
     dy = d_sum.third().astype(BF16).astype(F32)
     dx_sem = sems()
     for h in range(2):
-        back = dot(mix[h].T, dy[:, h * 128:(h + 1) * 128], **best)
+        back = dot(mix[h], dy[:, h * 128:(h + 1) * 128], **best)
         dxb[y, zl, :, pl.ds(h * 128, 128)] = (dtc[:, h:h + 1] * back).astype(BF16)
     send(dxb.at[y, zl], dxb.at[y, zl], dx_sem, flip_zl)
-    dx_ring.start([zl])
+    dx_ring.start([0])
     for j in range(3):
         arrived(lsc2.at[j], lc_sem + j)
     lring[y] = lsc[...] + lsc2[0] + lsc2[1] + lsc2[2]
     arrived(dxb.at[y, 1 - zl], dx_sem)
-    dx_ring.start([1 - zl])
+    dx_ring.start([1])
     loss_ring.start()
     arrived(hg.at[1 - c], hc_sem)
 
@@ -526,14 +529,16 @@
             arrived(lo_ref.at[:, pl.ds(k * 128, 128)], lo_sem + k)
 
 
-def store(lo_in, gx_in, loss_in, lo_out, gx_out, loss_out, sem):
-    moves = [
-        pltpu.make_async_copy(src, dst, sem.at[i])
-        for i, (src, dst) in enumerate(((gx_in, gx_out), (lo_in, lo_out), (loss_in, loss_out)))
-    ]
-    for move in moves:
+def store(lo_in, gx_in, loss_in, lo_out, gx_out, loss_out, lo, gx, loss, sem):
+    trips = ((gx_in, gx, gx_out), (lo_in, lo, lo_out), (loss_in, loss, loss_out))
+    reads = [pltpu.make_async_copy(a, b, sem.at[i]) for i, (a, b, _) in enumerate(trips)]
+    writes = [pltpu.make_async_copy(b, d, sem.at[3 + i]) for i, (_, b, d) in enumerate(trips)]
+    for move in reads:
         move.start()
-    for move in moves:
+    for read, write in zip(reads, writes):
+        read.wait()
+        write.start()
+    for move in writes:
         move.wait()
 
 
@@ -593,7 +598,9 @@
         ),
         in_specs=[anywhere] * 3,
         out_specs=(anywhere,) * 3,
-        scratch_shapes=[pltpu.SemaphoreType.DMA((3,))],
+        scratch_shapes=[
+            b(128, 256), f(512, 256), f(1, 1), pltpu.SemaphoreType.DMA((6,)),
+        ],
     )(layer_out, grad_x, loss)
     return layer_out, grad_x, loss[0, 0]
 

time: 162 us -> 134 us (0.83); the launches traced: 159 us -> 133 us
  Pallas kernels: 158 us -> 132 us
    pallas_call x1, Pallas kernels: 19.7 us -> 2.57 us  [local(): pl.pallas_call(store, out_shape=(jax.ShapeDtypeStruct((128, 256), BF16),...]
    pallas_call x1, Pallas kernels: 138 us -> 129 us  [local(): pl.pallas_call(kernel, out_shape=(jax.ShapeDtypeStruct((128, 256), BF16),...]
where the time goes in v3:
time: 134 us; the launch traced here: 133 us
  Pallas kernels  132 us (99%)
    pallas_call x1, Pallas kernels, local(): pl.pallas_call(kernel, out_shape=(jax.ShapeDtypeStruct((128, 256), BF16),...  129 us

profile of v3, /device:TPU:6, one launch (start us, length us, event | category | flops | bytes accessed | tf_op | source)
XLA Modules:
  0.0 132.7 jit_solution(18024538469377842634)
XLA Ops:
  0.6 129.5 %shard_map.121 = (bf16[128,256]{1,0:T(8,128)(2,1)}, f32[512,256]{1,0:T(8,128)}, f32[1,1]{1,0:T(1,128)}) custom-call(bf16[128,8192]{1,0:T(8,128)(2,1)} %hid_any.1, bf16[128,8192]{1,0:T(8,128)(2,1)} %tgt_any.1, s32[1,128]{1,0:T(1,128)} %seg_ref.1, s32[2]{0:T(128)} %map_ref.1, f32[2]{0:T(128)} %rate_ref.1, bf16[2,512]{1,0:T(2,128)(2,1)} %bitcast.10, ...), custom_call_target="tpu_custom_call" | custom-call | tf_op jit(solution)/shard_map/pallas_call | solution.py:575
  130.1 2.6 %shard_map.122 = (bf16[128,256]{1,0:T(8,128)(2,1)}, f32[512,256]{1,0:T(8,128)}, f32[1,1]{1,0:T(1,128)}) custom-call(bf16[128,256]{1,0:T(8,128)(2,1)} %get-tuple-element.9.lo_in, f32[512,256]{1,0:T(8,128)} %get-tuple-element.10.gx_in, f32[1,1]{1,0:T(1,128)} %get-tuple-element.11.loss_in), custom_call_target="tpu_custom_call" | custom-call | tf_op jit(solution)/shard_map/pallas_call | solution.py:592

commit v4 on v3

--- a/solution.py
+++ b/solution.py
@@ -188,14 +188,20 @@
 
     def rows_of(i):
         lanes = column(i)
-        return jnp.concatenate([hx[0, :, lanes], hx[1, :, lanes]], axis=0)
+        pieces = [hx[zz, pl.ds(hf * 64, 64), lanes] for hf in range(2) for zz in range(2)]
+        return jnp.concatenate(pieces, axis=0)
+
+    def q_add(j, value, fresh=False):
+        for hf in range(2):
+            half = value[hf * 128:(hf + 1) * 128]
+            cacc[hf, j] = half if fresh else cacc[hf, j] + half
 
     def q_pair(k):
         up, down = lax.rem(y + k, 8), lax.rem(y + 8 - k, 8)
         rows_up, rows_down = rows_of(up), rows_of(down)
         for j in range(4):
             lanes = pl.ds(j * 256, 256)
-            cacc[j] += dot(rows_up, qg[up, :, lanes]) + dot(rows_down, qg[down, :, lanes])
+            q_add(j, dot(rows_up, qg[up, :, lanes]) + dot(rows_down, qg[down, :, lanes]))
 
     arrived(hx.at[1 - zl], h_sem)
     arrived(dtb.at[y, pl.ds(pl.multiple_of((1 - zl) * 8, 8), 8)], dt_sem)
@@ -204,7 +210,7 @@
     send(other_target, tg.at[zl], t_sem, flip_zl)
     rows = rows_of(y)
     for j in range(4):
-        cacc[j] = dot(rows, qg[y, :, pl.ds(j * 256, 256)])
+        q_add(j, dot(rows, qg[y, :, pl.ds(j * 256, 256)]), True)
     q_ring.step(1, [0])
     kv_ring.step(2)
     q_ring.step(1, [1])
@@ -254,24 +260,32 @@
         send(own_kv, own_kv, k3_sem + d - 1, s_dev(lax.rem(s + d, 8)))
 
     class Sum8:
-        def __init__(self, acc, p1, r1, p2, r2):
+        def __init__(self, acc, p1, r1, p2, r2, rows):
             self.acc, self.p1, self.r1, self.p2, self.r2 = acc, p1, r1, p2, r2
+            self.rows = rows
             self.s1, self.s2 = sems(), sems(3)
 
-        def first(self, add):
+        def first(self, add, fresh=False):
+            n = self.rows
             for hh in range(2):
-                part = self.acc[hh * 2 + 1 - c] + add(hh * 2 + 1 - c)
+                part = add(hh * 2 + 1 - c)
+                if not fresh:
+                    part += self.acc[hh * 2 + 1 - c]
                 for zz in range(2):
-                    self.p1[zz, hh] = part[zz * 128:(zz + 1) * 128].astype(BF16)
+                    self.p1[zz, hh] = part[zz * n:(zz + 1) * n].astype(BF16)
             send(self.p1, self.r1, self.s1, flip_c)
             for hh in range(2):
-                self.acc[hh * 2 + c] += add(hh * 2 + c)
+                if fresh:
+                    self.acc[hh * 2 + c] = add(hh * 2 + c)
+                else:
+                    self.acc[hh * 2 + c] += add(hh * 2 + c)
 
         def second(self):
+            n = self.rows
             arrived(self.r1, self.s1)
             for zz in range(2):
                 for hh in range(2):
-                    rows = pl.ds(zz * 128, 128)
+                    rows = pl.ds(zz * n, n)
                     part = self.acc[hh * 2 + c, rows, :] + self.r1[zz, hh].astype(F32)
                     self.acc[hh * 2 + c, rows, :] = part
                     self.p2[zz, hh] = part.astype(BF16)
@@ -280,24 +294,29 @@
             send(self.p2.at[1 - zl, zh0], self.r2.at[1], self.s2 + 1, flip_zl)
 
         def third(self):
+            n = self.rows
             for j in range(3):
                 arrived(self.r2.at[j], self.s2 + j)
-            own = self.acc[zh0 * 2 + c, pl.ds(pl.multiple_of(zl * 128, 128), 128), :]
+            own = self.acc[zh0 * 2 + c, pl.ds(pl.multiple_of(zl * n, n), n), :]
             return own + self.r2[0].astype(F32) + self.r2[1].astype(F32) + self.r2[2].astype(F32)
 
-    c_sum = Sum8(cacc, cp1, cr1, cp2, cr2)
-    d_sum = Sum8(dacc, dp1, dr1, dp2, dr2)
+    c_sums = [
+        Sum8(cacc.at[hf], cp1.at[hf], cr1.at[hf], cp2.at[hf], cr2.at[hf], 64) for hf in range(2)
+    ]
 
     last = [lax.rem(y + k, 8) for k in (3, 4, 5)]
     last_rows = [rows_of(i) for i in last]
-
-    def last_q(k):
-        lanes = pl.ds(pl.multiple_of(k * 256, 256), 256)
-        return sum(dot(r, qg[i, :, lanes]) for r, i in zip(last_rows, last))
-
-    c_sum.first(last_q)
+    for hf in range(2):
+
+        def last_q(k):
+            lanes = pl.ds(pl.multiple_of(k * 256, 256), 256)
+            rows = slice(hf * 128, (hf + 1) * 128)
+            return sum(dot(r[rows], qg[i, :, lanes]) for r, i in zip(last_rows, last))
+
+        c_sums[hf].first(last_q)
     o_ring.step(0, [0])
-    c_sum.second()
+    c_sums[0].second()
+    c_sums[1].second()
     dt_ring.step(3)
     o_ring.step(0, [1])
     w2[...] = jnp.zeros_like(w2)
@@ -338,89 +357,115 @@
     for d in range(1, 8):
         arrived(kvall.at[c, lax.rem(s + 8 - d, 8)], k3_sem + d - 1)
     send(kvall.at[c], kvall.at[c], k4_sem, flip_c)
-    y_sem, y2_sem = sems(3), sems()
-    c_full = (c_sum.third() * (128 ** -0.5)).astype(BF16)
+    y_sem, y2_sem = sems(6), sems(2)
     arrived(kvall.at[1 - c], k4_sem)
-    mixings = []
+    keys, sources = [], []
     for h in range(2):
         head = map_ref[h]
         both = jnp.concatenate([kvall[0, head], kvall[1, head]], axis=0)
-        scores = dot_t(c_full[:, h * 128:(h + 1) * 128], both[:, :128])
-        mixing = scores * mix[h]
-        mixings.append(mixing)
-        source = dtc[:, h:h + 1] * both[:, 128:].astype(F32)
-        yb[c, zl, zh0, :, pl.ds(h * 128, 128)] = dot(mixing, source, **best).astype(BF16)
-    own_y = yb.at[c, zl, zh0]
-    send(own_y, own_y, y_sem + 2, flip_zh)
-    send(own_y, own_y, y_sem, flip_h)
-    send(own_y, own_y, y_sem + 1, flip_zl)
+        keys.append(both[:, :128])
+        sources.append(dtc[:, h:h + 1] * both[:, 128:].astype(F32))
+
+    def y_rows(hf, zz, hh):
+        return yb.at[c, zz, hh, pl.ds(hf * 64, 64)]
+
+    for hf in range(2):
+        rows = pl.ds(hf * 64, 64)
+        c_half = (c_sums[hf].third() * (128 ** -0.5)).astype(BF16)
+        for h in range(2):
+            lanes = slice(h * 128, (h + 1) * 128)
+            mixing = dot_t(c_half[:, lanes], keys[h]) * mix[h, rows]
+            mix[h, rows] = mixing
+            yb[c, zl, zh0, rows, pl.ds(h * 128, 128)] = dot(
+                mixing, sources[h], **best
+            ).astype(BF16)
+        own_y = y_rows(hf, zl, zh0)
+        send(own_y, own_y, y_sem + hf * 3 + 2, flip_zh)
+        send(own_y, own_y, y_sem + hf * 3, flip_h)
+        send(own_y, own_y, y_sem + hf * 3 + 1, flip_zl)
     for h in range(2):
-        mix[h] = mixings[h].T
+        mix[h] = mix[h].T
     o_ring.step(2)
-    arrived(yb.at[c, zl, 1 - zh0], y_sem)
-    arrived(yb.at[c, 1 - zl, zh0], y_sem + 1)
-    arrived(yb.at[c, 1 - zl, 1 - zh0], y_sem + 2)
-    send(yb.at[c], yb.at[c], y2_sem, flip_c)
+    for hf in range(2):
+        arrived(y_rows(hf, zl, 1 - zh0), y_sem + hf * 3)
+        arrived(y_rows(hf, 1 - zl, zh0), y_sem + hf * 3 + 1)
+        arrived(y_rows(hf, 1 - zl, 1 - zh0), y_sem + hf * 3 + 2)
+        both_y = yb.at[c, :, :, pl.ds(hf * 64, 64)]
+        send(both_y, both_y, y2_sem + hf, flip_c)
     hc_sem = sems()
     o_ring.step(3)
-    arrived(yb.at[1 - c], y2_sem)
+
+    def y_all(hf):
+        arrived(yb.at[1 - c, :, :, pl.ds(hf * 64, 64)], y2_sem + hf)
+        for zz in range(2):
+            for hh in range(2):
+                for cc in range(2):
+                    rows = pl.ds(hf * 128 + zz * 64, 64)
+                    lanes = pl.ds((hh * 2 + cc) * 256, 256)
+                    ycat[rows, lanes] = yb[cc, zz, hh, pl.ds(hf * 64, 64)]
+
+    halves = range(2)
+    l0_sem, l1_sem, l2_sem = sems(6), sems(6), sems(2)
+    for hf in halves:
+        y_all(hf)
+        for d in (2, 1, 3, 0):
+            at = lax.rem(x + d, 4)
+            lanes = pl.ds(pl.multiple_of(at * 256, 256), 256)
+            value = dot(ycat[pl.ds(hf * 128, 128), :], og[:, lanes])
+            if d:
+                i = hf * 3 + d - 1
+                lp[hf, at, 0] = value[:, :128].astype(BF16)
+                lp[hf, at, 1] = value[:, 128:].astype(BF16)
+                send(lp.at[hf, at, 1 - zh1], lr1.at[hf, 1, d - 1], l0_sem + i, x_dev(d))
+            else:
+                lt[hf, 0] = value[:, :128]
+                lt[hf, 1] = value[:, 128:]
+    for hf in halves:
+        for d in (2, 1, 3):
+            at = lax.rem(x + d, 4)
+            send(lp.at[hf, at, zh1], lr1.at[hf, 0, d - 1], l1_sem + hf * 3 + d - 1, x_dev(d))
+    for hf in halves:
+        part = lt[hf, 1 - zh1]
+        for d in range(3):
+            arrived(lr1.at[hf, 1, d], l0_sem + hf * 3 + d)
+            part += lr1[hf, 1, d].astype(F32)
+        ls[hf] = part.astype(BF16)
+        send(ls.at[hf], lr2.at[hf], l2_sem + hf, flip_h1)
     for d in range(1, 4):
         arrived(hg.at[c, pl.ds(lax.rem(x + 4 - d, 4) * 4, 4)], hx_sem + d - 1)
     send(hg.at[c], hg.at[c], hc_sem, flip_c)
-    for zz in range(2):
-        for hh in range(2):
-            for cc in range(2):
-                ycat[pl.ds(zz * 128, 128), pl.ds((hh * 2 + cc) * 256, 256)] = yb[cc, zz, hh]
-
-    l0_sem, l1_sem, l2_sem = sems(3), sems(3), sems()
-    for d in (2, 1, 3, 0):
-        at = lax.rem(x + d, 4)
-        value = dot(ycat[...], og[:, pl.ds(pl.multiple_of(at * 256, 256), 256)])
-        if d:
-            lp[at, 0] = value[:, :128].astype(BF16)
-            lp[at, 1] = value[:, 128:].astype(BF16)
-            send(lp.at[at, 1 - zh1], lr1.at[1, d - 1], l0_sem + d - 1, x_dev(d))
-        else:
-            lt[0] = value[:, :128]
-            lt[1] = value[:, 128:]
-    for d in (2, 1, 3):
-        at = lax.rem(x + d, 4)
-        send(lp.at[at, zh1], lr1.at[0, d - 1], l1_sem + d - 1, x_dev(d))
-    for d in range(3):
-        arrived(lr1.at[1, d], l0_sem + d)
-    ls[...] = (
-        lt[1 - zh1] + lr1[1, 0].astype(F32) + lr1[1, 1].astype(F32) + lr1[1, 2].astype(F32)
-    ).astype(BF16)
-    send(ls, lr2, l2_sem, flip_h1)
-    for d in range(3):
-        arrived(lr1.at[0, d], l1_sem + d)
-    near = lt[zh1] + lr1[0, 0].astype(F32) + lr1[0, 1].astype(F32) + lr1[0, 2].astype(F32)
     target_in.wait()
     arrived(tg.at[1 - zl], t_sem)
-    arrived(lr2, l2_sem)
-    layer = (near + lr2[...].astype(F32)).astype(BF16)
-    g1_sem, g2_sem, g3_sem, la_sem, la2_sem = sems(), sems(3), sems(3), sems(), sems(3)
+    g1_sem, g2_sem, g3_sem, la_sem, la2_sem = sems(2), sems(6), sems(6), sems(), sems(3)
     squares = jnp.zeros((8, 128), F32)
-    for zz in range(2):
-        rows = layer[zz * 128:(zz + 1) * 128]
-        lob[zz] = rows
-        residual = rows.astype(F32) - tg[zz].astype(F32)
-        gob[pl.ds(zz * 128, 128), column(s)] = (2.0 * residual / TOKENS).astype(BF16)
-        squares += jnp.sum((residual * residual).reshape(16, 8, 128), axis=0)
+
+    def g_piece(hf, index):
+        return gob.at[pl.ds(hf * 128, 128), column(index)]
+
+    for hf in halves:
+        part = lt[hf, zh1]
+        for d in range(3):
+            arrived(lr1.at[hf, 0, d], l1_sem + hf * 3 + d)
+            part += lr1[hf, 0, d].astype(F32)
+        arrived(lr2.at[hf], l2_sem + hf)
+        layer = (part + lr2[hf].astype(F32)).astype(BF16)
+        for zz in range(2):
+            rows = layer[zz * 64:(zz + 1) * 64]
+            lob[zz, pl.ds(hf * 64, 64)] = rows
+            residual = rows.astype(F32) - tg[zz, pl.ds(hf * 64, 64)].astype(F32)
+            gob[pl.ds(hf * 128 + zz * 64, 64), column(s)] = (2.0 * residual / TOKENS).astype(BF16)
+            squares += jnp.sum((residual * residual).reshape(8, 8, 128), axis=0)
+        own_g = g_piece(hf, s)
+        send(own_g, own_g, g1_sem + hf, flip_h1)
+        for d in (2, 1, 3):
+            send(own_g, own_g, g2_sem + hf * 3 + d - 1, x_dev(d))
     lsa[s] = squares
-    own_g = gob.at[:, column(s)]
-    send(own_g, own_g, g1_sem, flip_h1)
-    for d in (2, 1, 3):
-        send(own_g, own_g, g2_sem + d - 1, x_dev(d))
     send(lsa.at[s], lsa.at[s], la_sem, flip_h1)
-    next_g = gob.at[:, column(2 * x + 1 - zh1)]
-    arrived(next_g, g1_sem)
-    for d in (2, 1, 3):
-        send(next_g, next_g, g3_sem + d - 1, x_dev(d))
-    arrived(lsa.at[2 * x + 1 - zh1], la_sem)
-    loss_pair = lsa.at[pl.ds(x * 2, 2)]
-    for d in range(1, 4):
-        send(loss_pair, loss_pair, la2_sem + d - 1, x_dev(d))
+    for hf in halves:
+        next_g = g_piece(hf, 2 * x + 1 - zh1)
+        arrived(next_g, g1_sem + hf)
+        for d in (2, 1, 3):
+            send(next_g, next_g, g3_sem + hf * 3 + d - 1, x_dev(d))
 
     lo_sem = sems(2)
     lo_tn = 16 * zl + 2 * s + lax.div(q, 2)
@@ -444,27 +489,27 @@
         def _():
             copy.start()
 
-    def d_part(at):
-        lanes = pl.ds(pl.multiple_of(at * 256, 256), 256)
-        rows = gob[:, lanes]
+    arrived(lsa.at[2 * x + 1 - zh1], la_sem)
+    loss_pair = lsa.at[pl.ds(x * 2, 2)]
+    for d in range(1, 4):
+        send(loss_pair, loss_pair, la2_sem + d - 1, x_dev(d))
+    d_sums = [
+        Sum8(dacc.at[hf], dp1.at[hf], dr1.at[hf], dp2.at[hf], dr2.at[hf], 64) for hf in halves
+    ]
+    for hf in halves:
+        for d in (1, 3, 2):
+            at = lax.rem(x + 4 - d, 4)
+            arrived(g_piece(hf, at * 2 + zh1), g2_sem + hf * 3 + d - 1)
+            arrived(g_piece(hf, at * 2 + 1 - zh1), g3_sem + hf * 3 + d - 1)
+        rows = gob[pl.ds(hf * 128, 128), :]
 
         def part(k):
-            return dot_t(rows, og[pl.ds(pl.multiple_of(k * 256, 256), 256), lanes])
-        return part
-
-    part = d_part(x)
-    for k in range(4):
-        dacc[k] = part(k)
-    for d in (1, 3, 2):
-        at = lax.rem(x + 4 - d, 4)
-        arrived(gob.at[:, column(at * 2 + zh1)], g2_sem + d - 1)
-        arrived(gob.at[:, column(at * 2 + 1 - zh1)], g3_sem + d - 1)
-        part = d_part(at)
-        if d == 2:
-            d_sum.first(part)
-        else:
-            for k in range(4):
-                dacc[k] += part(k)
+            return dot_t(rows, og[pl.ds(pl.multiple_of(k * 256, 256), 256), :])
+
+        d_sums[hf].first(part, True)
+        if hf:
+            d_sums[0].second()
+    d_sums[1].second()
     lb_sem, lc_sem = sems(), sems(3)
     for d in range(1, 4):
         arrived(lsa.at[pl.ds(lax.rem(x + 4 - d, 4) * 2, 2)], la2_sem + d - 1)
@@ -473,12 +518,12 @@
         total += lsa[i]
     lsb[...] = total
     send(lsb, lsb1, lb_sem, flip_c)
-    d_sum.second()
     arrived(lsb1, lb_sem)
     lsc[...] = lsb[...] + lsb1[...]
     for j in range(3):
         send(lsc, lsc2.at[j], lc_sem + j, line[j])
-    dy = d_sum.third().astype(BF16).astype(F32)
+    dy = jnp.concatenate([d_sums[hf].third() for hf in halves], axis=0)
+    dy = dy.astype(BF16).astype(F32)
     dx_sem = sems()
     for h in range(2):
         back = dot(mix[h], dy[:, h * 128:(h + 1) * 128], **best)
@@ -562,12 +607,13 @@
         f(8, 16, 128), b(2, 128, 1024), b(128, 1024), b(256, 128), b(2, 16, 256, 128),
         f(256, 256), b(2, 64, 256), b(2, 64, 256), f(2, 64, 256), b(2, 64, 256), b(3, 64, 256),
         b(2, 8, 64, 256),
-        f(4, 256, 256), b(2, 2, 128, 256), b(2, 2, 128, 256), b(2, 2, 128, 256), b(3, 128, 256),
+        f(2, 4, 128, 256), b(2, 2, 2, 64, 256), b(2, 2, 2, 64, 256), b(2, 2, 2, 64, 256),
+        b(2, 3, 64, 256),
         f(16, 8192), f(2, 128, 128), f(128, 16), b(2, 2, 2, 128, 256), b(256, 1024),
-        b(4, 2, 256, 128), b(2, 3, 256, 128), f(2, 256, 128), b(256, 128),
-        b(256, 128), b(2, 128, 128),
-        b(256, 1024), f(4, 256, 256), b(2, 2, 128, 256), b(2, 2, 128, 256),
-        b(2, 2, 128, 256), b(3, 128, 256), b(8, 2, 128, 256),
+        b(2, 4, 2, 128, 128), b(2, 2, 3, 128, 128), f(2, 2, 128, 128), b(2, 128, 128),
+        b(2, 128, 128), b(2, 128, 128),
+        b(256, 1024), f(2, 4, 128, 256), b(2, 2, 2, 64, 256), b(2, 2, 2, 64, 256),
+        b(2, 2, 2, 64, 256), b(2, 3, 64, 256), b(8, 2, 128, 256),
         f(8, 8, 128), f(8, 128), f(8, 128), f(8, 128), f(3, 8, 128), f(8, 8, 128),
         pltpu.SemaphoreType.DMA((N_SEM,)), pltpu.SemaphoreType.DMA((N_SEM,)),
         pltpu.SemaphoreType.DMA((6,)),

time: 134 us -> 130 us (0.970)
  Pallas kernels: 132 us -> 127 us
    pallas_call x1, Pallas kernels: 129 us -> 124 us  [local(): pl.pallas_call(kernel, out_shape=(jax.ShapeDtypeStruct((128, 256), BF16),...]
where the time goes in v4:
time: 130 us; the launch traced here: 128 us
  Pallas kernels  127 us (98%)
    pallas_call x1, Pallas kernels, local(): pl.pallas_call(kernel, out_shape=(jax.ShapeDtypeStruct((128, 256), BF16),...  124 us

profile of v4, /device:TPU:6, one launch (start us, length us, event | category | flops | bytes accessed | tf_op | source)
XLA Modules:
  0.0 127.5 jit_solution(16939202223038592793)
XLA Ops:
  0.6 124.3 %shard_map.121 = (bf16[128,256]{1,0:T(8,128)(2,1)}, f32[512,256]{1,0:T(8,128)}, f32[1,1]{1,0:T(1,128)}) custom-call(bf16[128,8192]{1,0:T(8,128)(2,1)} %hid_any.1, bf16[128,8192]{1,0:T(8,128)(2,1)} %tgt_any.1, s32[1,128]{1,0:T(1,128)} %seg_ref.1, s32[2]{0:T(128)} %map_ref.1, f32[2]{0:T(128)} %rate_ref.1, bf16[2,512]{1,0:T(2,128)(2,1)} %bitcast.10, ...), custom_call_target="tpu_custom_call" | custom-call | tf_op jit(solution)/shard_map/pallas_call | solution.py:621
  124.9 2.6 %shard_map.122 = (bf16[128,256]{1,0:T(8,128)(2,1)}, f32[512,256]{1,0:T(8,128)}, f32[1,1]{1,0:T(1,128)}) custom-call(bf16[128,256]{1,0:T(8,128)(2,1)} %get-tuple-element.9.lo_in, f32[512,256]{1,0:T(8,128)} %get-tuple-element.10.gx_in, f32[1,1]{1,0:T(1,128)} %get-tuple-element.11.loss_in), custom_call_target="tpu_custom_call" | custom-call | tf_op jit(solution)/shard_map/pallas_call | solution.py:638

commit v5 on v4

--- a/solution.py
+++ b/solution.py
@@ -156,10 +156,10 @@
                         if k < 3 and self.live(k + 1, d, ch):
                             self.send(k + 1, d, ch)
 
-    kv_ring = Ring(lambda b, ch: kvg.at[b, pl.ds(ch * 64, 64)], 2)
+    kv_ring = Ring(lambda b, ch: kvg.at[b], 1)
     q_ring = Ring(lambda b, ch: qg.at[b, pl.ds(ch * 64, 64)], 2)
     o_ring = Ring(lambda b, ch: og.at[pl.ds(ch * 512, 512), column(b)], 2)
-    dt_ring = Ring(lambda b, ch: dtb.at[b, pl.ds(ch * 8, 8)], 2)
+    dt_ring = Ring(lambda b, ch: dtb.at[b], 1)
     dx_ring = Ring(lambda b, ch: dxb.at[b, 1 - zl if ch else zl], 2)
     loss_ring = Ring(lambda b, ch: lring.at[b], 1)
 

time: 130 us -> 129 us (level)
  no operation moved by 1% of the time
where the time goes in v5:
time: 129 us; the launch traced here: 128 us
  Pallas kernels  127 us (98%)
    pallas_call x1, Pallas kernels, local(): pl.pallas_call(kernel, out_shape=(jax.ShapeDtypeStruct((128, 256), BF16),...  124 us

profile of v5, /device:TPU:6, one launch (start us, length us, event | category | flops | bytes accessed | tf_op | source)
XLA Modules:
  0.0 127.6 jit_solution(5144192685868202769)
XLA Ops:
  0.6 124.4 %shard_map.121 = (bf16[128,256]{1,0:T(8,128)(2,1)}, f32[512,256]{1,0:T(8,128)}, f32[1,1]{1,0:T(1,128)}) custom-call(bf16[128,8192]{1,0:T(8,128)(2,1)} %hid_any.1, bf16[128,8192]{1,0:T(8,128)(2,1)} %tgt_any.1, s32[1,128]{1,0:T(1,128)} %seg_ref.1, s32[2]{0:T(128)} %map_ref.1, f32[2]{0:T(128)} %rate_ref.1, bf16[2,512]{1,0:T(2,128)(2,1)} %bitcast.10, ...), custom_call_target="tpu_custom_call" | custom-call | tf_op jit(solution)/shard_map/pallas_call | solution.py:621
  125.0 2.6 %shard_map.122 = (bf16[128,256]{1,0:T(8,128)(2,1)}, f32[512,256]{1,0:T(8,128)}, f32[1,1]{1,0:T(1,128)}) custom-call(bf16[128,256]{1,0:T(8,128)(2,1)} %get-tuple-element.9.lo_in, f32[512,256]{1,0:T(8,128)} %get-tuple-element.10.gx_in, f32[1,1]{1,0:T(1,128)} %get-tuple-element.11.loss_in), custom_call_target="tpu_custom_call" | custom-call | tf_op jit(solution)/shard_map/pallas_call | solution.py:638
